TPU v7x, 32 devices: a whole 2x2x4 slice. The times are simulated.
32 devices in a mesh: ctx: 16 (over z, x, core), ch: 2 (over y).
Axes of the slice: x: 2, y: 2, z: 4, core: 2. Of those that a mesh axis runs over, the one named last changes fastest.
Arguments:
- qkv: bfloat16 [3, 512, 4096], P(None, None, ('ctx', 'ch')), may hold values from -6 to 6
- conv_taps: float32 [3, 512, 7], replicated, may hold values from -2 to 2
- filters: float32 [512, 4096], P('ch', 'ctx'), may hold values from -0.09375 to 0.09375
- skip: float32 [512], P('ch'), may hold values from -4 to 4
Outputs:
- mixed: bfloat16 [512, 4096], P('ch', 'ctx')
All inputs are finite; a program needn't handle non-finite values.
Results may differ from a plain program's by a relative error of at most 0.013.
Values may be sent and summed in bfloat16 or wider, within the bound.
A program may use at most 64 MiB of HBM per device.

v0:
```python
import math

import jax
import jax.numpy as jnp
from jax import lax
from jax.sharding import PartitionSpec as P


def from_behind(shard, axis, by):
    length = lax.axis_size(axis)
    pairs = [(i, i + by) for i in range(length) if 0 <= i + by < length]
    return lax.ppermute(shard, axis, pairs)


def featurize(block, earlier, taps):
    reach = taps.shape[2] - 1
    length = block.shape[2]
    joined = jnp.concatenate([earlier, block], axis=2).astype(jnp.float32)
    total = jnp.zeros(block.shape, jnp.float32)
    for offset in range(taps.shape[2]):
        total = (
            total
            + taps[:, :, offset : offset + 1]
            * joined[:, :, reach - offset : reach - offset + length]
        )
    query = lax.optimization_barrier(total[0].astype(jnp.bfloat16))
    gated = lax.optimization_barrier((total[1] * total[2]).astype(jnp.bfloat16))
    return (query, gated)


def phase(product, modulus, sign):
    angle = sign * 2.0 * math.pi / modulus * (product % modulus).astype(jnp.float32)
    return (jnp.cos(angle), jnp.sin(angle))


def dft_table(index_in, index_out, modulus, sign):
    cosine, sine = phase(index_in[:, None] * index_out[None, :], modulus, sign)
    return jnp.stack([jnp.stack([cosine, sine]), jnp.stack([-sine, cosine])])


def complex_times(left, right):
    return jnp.stack(
        [left[0] * right[0] - left[1] * right[1], left[0] * right[1] + left[1] * right[0]]
    )


def twisted(values, cosine, sine):
    return jnp.stack([values[0] * cosine - values[1] * sine, values[0] * sine + values[1] * cosine])


def local_transform(values, sign):
    highest = lax.Precision.HIGHEST
    length = values.shape[-1]
    first = max((d for d in range(1, math.isqrt(length) + 1) if length % d == 0))
    second = length // first
    lead = values.shape[:-1]
    shaped = values.reshape(lead + (first, second))
    index_a = jnp.arange(first, dtype=jnp.int32)
    index_b = jnp.arange(second, dtype=jnp.int32)
    outer = dft_table(index_a, index_a, first, sign)
    part = jnp.einsum("p...ab,pqak->q...kb", shaped, outer, precision=highest)
    twist_c, twist_s = phase(index_a[:, None] * index_b[None, :], length, sign)
    part = twisted(part, twist_c, twist_s)
    inner = dft_table(index_b, index_b, second, sign)
    result = jnp.einsum("p...kb,pqbm->q...mk", part, inner, precision=highest)
    return result.reshape(lead + (length,))


def to_columns(values):
    return lax.all_to_all(
        values.astype(jnp.bfloat16), "ctx", split_axis=3, concat_axis=2, tiled=True
    ).astype(values.dtype)


def to_rows(values):
    return lax.all_to_all(
        values.astype(jnp.bfloat16), "ctx", split_axis=2, concat_axis=3, tiled=True
    ).astype(values.dtype)


def spread_conv(signal, filters):
    highest = lax.Precision.HIGHEST
    lanes = lax.axis_size("ctx")
    block = signal.shape[1]
    piece = block // lanes
    total_len = 2 * lanes * block
    mine = lax.axis_index("ctx")
    order = jnp.arange(2 * lanes, dtype=jnp.int32)
    owner = order // 2
    parity = order % 2
    freq_rows = jnp.where(
        owner == 0, parity * lanes, jnp.where(parity == 0, owner, 2 * lanes - owner)
    )
    own_rows = lax.dynamic_slice_in_dim(freq_rows, 2 * mine, 2)
    sources = jnp.arange(lanes, dtype=jnp.int32)
    cross = dft_table(sources, freq_rows, 2 * lanes, -1.0)
    column_pos = mine * piece + jnp.arange(piece, dtype=jnp.int32)
    twist_c, twist_s = phase(freq_rows[:, None] * column_pos[None, :], total_len, -1.0)
    columns = to_columns(jnp.stack([signal, filters])[:, :, None, :])
    spec = jnp.einsum("scaj,qar->qscrj", columns, cross[0], precision=highest)
    spec = twisted(spec, twist_c, twist_s)
    width_dev = spec.shape[2]
    arrived = to_rows(spec.reshape((4, width_dev) + spec.shape[3:]))
    arrived = arrived.reshape((2, 2, width_dev) + arrived.shape[2:])
    freq = local_transform(arrived, -1.0)
    prod = complex_times(freq[:, 0], freq[:, 1])
    back = local_transform(prod, 1.0)
    full_pos = jnp.arange(block, dtype=jnp.int32)
    turn_c, turn_s = phase(own_rows[:, None] * full_pos[None, :], total_len, 1.0)
    back = twisted(back, turn_c, turn_s)
    spread = to_columns(back)
    merge = dft_table(freq_rows, sources, 2 * lanes, 1.0)
    partial_out = jnp.einsum("pcrj,pra->caj", spread, merge[:, 0], precision=highest)
    landed = to_rows(partial_out[None])
    return landed[0, :, 0, :] / total_len


def local(qkv, conv_taps, filters, skip):
    reach = conv_taps.shape[2] - 1
    grouped = lax.all_to_all(qkv, "ch", split_axis=1, concat_axis=2, tiled=True)
    earlier = from_behind(grouped[:, :, -reach:], "ctx", 1)
    width_dev = grouped.shape[1]
    taps_mine = lax.dynamic_slice_in_dim(conv_taps, lax.axis_index("ch") * width_dev, width_dev, 1)
    query, gated = featurize(grouped, earlier, taps_mine)
    signal = gated.astype(jnp.float32)
    long_conv = spread_conv(signal, filters)
    mixed = query.astype(jnp.float32) * (long_conv + skip[:, None] * signal)
    return mixed.astype(jnp.bfloat16)


def solution(mesh):
    return jax.shard_map(
        local,
        mesh=mesh,
        in_specs=(P(None, None, ("ctx", "ch")), P(), P("ch", "ctx"), P("ch")),
        out_specs=P("ch", "ctx"),
        check_vma=False,
    )
```

profile of v0, /device:TPU:0, one launch (start us, length us, event | category | flops | bytes accessed | tf_op | source)
XLA Modules:
  0.0 116.2 jit_solution(14284286617084499350)
XLA Ops:
  0.0 2.2 %copy.50 = bf16[3,512,128]{2,0,1:T(4,128)(2,1)} copy(bf16[3,512,128]{2,1,0:T(8,128)(2,1)} %param.4) | data formatting | bytes 786432 | tf_op args[0]
  2.2 4.2 %all-to-all-start = ((bf16[3,512,128]{2,0,1:T(4,128)(2,1)}), bf16[3,512,128]{2,0,1:T(4,128)(2,1)S(1)}, u32[]{:S(2)}, u32[]{:S(2)}) async-start(bf16[3,512,128]{2,0,1:T(4,128)(2,1)} %copy.50), calls=%async_computation | async-start | bytes 1048576 | tf_op jit(solution)/shard_map/all_to_all | solution.py:120
  6.4 1.2 %constant_dynamic-slice_fusion.5 = (f32[3,256,1]{1,2,0:T(1,128)S(1)}, f32[3,256,1]{1,2,0:T(1,128)S(1)}, f32[3,256,1]{1,2,0:T(1,128)S(1)}, f32[3,256,1]{1,2,0:T(1...) fusion(f32[3,512,7]{1,2,0:T(8,128)} %param.5, s32[]{:T(128)S(6)} %select_n.269, ...), kind=kLoop, calls=%fused_computation.162 | loop fusion | bytes 43036 | tf_op jit(solution)/shard_map/slice | solution.py:23
  7.7 7.5 %all-to-all-done = bf16[3,512,128]{2,0,1:T(4,128)(2,1)S(1)} async-done(((bf16[3,512,128]{2,0,1:T(4,128)(2,1)}), bf16[3,512,128]{2,0,1:T(4,128)(2,1)S(1)}, u32[]{:S(2)}, u32[]{:S(2)}) %all-to-all-start) | async-done | bytes 393248 | tf_op jit(solution)/shard_map/all_to_all | solution.py:120
  15.4 1.3 %collective-permute-start = (bf16[3,256,6]{1,2,0:T(8,128)(2,1)S(1)}, bf16[3,256,6]{1,2,0:T(8,128)(2,1)S(1)}, u32[]{:S(2)}, u32[]{:S(2)}) collective-permute-start(bf16[3,256,6]{1,2,0:T(8,128)(2,1)S(1)} %slice.149), channel_id=1, source_target_pairs={{0,2},{2,4},{4,6},{6,8},{8,10},{10,12},{12,14},{14,16},{16,18},{18... | collective-permute-start | bytes 27656 | tf_op jit(solution)/shard_map/ppermute | solution.py:12
  16.9 0.7 collective-permute-done
  17.6 0.6 fusion.14
  18.4 1.0 copy.55
  19.3 9.0 %all-to-all-start.1 = ((bf16[2,256,1,256]{1,0,2,3:T(2,128)(2,1)}), bf16[2,256,1,256]{1,0,2,3:T(2,128)(2,1)S(1)}, u32[]{:S(2)}, u32[]{:S(2)}) async-start(bf16[2,256,1,256]{1,0,2,3:T(2,128)(2,1)} %copy.55), calls=%async_computation.1 | async-start | bytes 524288 | tf_op jit(solution)/shard_map/all_to_all | solution.py:70
  28.6 9.8 %all-to-all-done.1 = bf16[2,256,1,256]{1,0,2,3:T(2,128)(2,1)S(1)} async-done(((bf16[2,256,1,256]{1,0,2,3:T(2,128)(2,1)}), bf16[2,256,1,256]{1,0,2,3:T(2,128)(2,1)S(1)}, u32[]{:S(2)}, u32[]{:S(2)}) %all-to-all-start.1) | async-done | bytes 262176 | tf_op jit(solution)/shard_map/all_to_all | solution.py:70
  38.4 1.0 convolution_bitcast_fusion.1
  39.4 0.3 subtract_convert_fusion
  39.9 1.6 %copy.58 = bf16[4,256,32,16]{1,3,0,2:T(8,128)(2,1)} copy(bf16[4,256,32,16]{1,2,3,0:T(8,128)(2,1)S(1)} %bitcast.159) | data formatting | bytes 2097152 | tf_op jit(solution)/shard_map/convert_element_type | solution.py:77
  41.4 3.8 %all-to-all-start.2 = ((bf16[4,256,32,16]{1,3,0,2:T(8,128)(2,1)}), bf16[4,256,32,16]{1,3,0,2:T(8,128)(2,1)S(1)}, u32[]{:S(2)}, u32[]{:S(2)}) async-start(bf16[4,256,32,16]{1,3,0,2:T(8,128)(2,1)} %copy.58), calls=%async_computation.2 | async-start | bytes 2097152 | tf_op jit(solution)/shard_map/all_to_all | solution.py:76
  45.9 22.1 %all-to-all-done.2 = bf16[4,256,32,16]{1,3,0,2:T(8,128)(2,1)S(1)} async-done(((bf16[4,256,32,16]{1,3,0,2:T(8,128)(2,1)}), bf16[4,256,32,16]{1,3,0,2:T(8,128)(2,1)S(1)}, u32[]{:S(2)}, u32[]{:S(2)}) %all-to-all-start.2) | async-done | bytes 1048608 | tf_op jit(solution)/shard_map/all_to_all | solution.py:76
  68.0 1.3 %convolution_bitcast_fusion = f32[2,2,256,2,16,16]{2,4,5,3,1,0:T(8,128)S(1)} fusion(bf16[2,2,256,2,16,16]{2,5,1,0,3,4:T(8,128)(2,1)S(1)} %bitcast.158, f32[1,2,16,16]{2,3,0,1:T(8,128)S(1)} %get-tuple-element.29, f32[1,2,16,16]{2,3,0,1:T(8,128)S(1)} %get-tuple-element.28), kind=kOutput, calls=%fused_computation.5 | convolution fusion | flops 201327616 | bytes 3149824 | tf_op jit(solution)/shard_map/p...ab,pqak->q...kb/dot_general | solution.py:61
  69.3 0.4 multiply_subtract_fusion
  69.8 3.0 %fusion.3 = f32[2,2,256,2,16,16]{2,4,5,3,1,0:T(8,128)S(1)} fusion(f32[2,2,256,2,16,16]{2,4,5,3,1,0:T(8,128)S(1)} %pad_maximum_fusion, f32[1,2,16,16]{2,3,0,1:T(8,128)S(1)} %get-tuple-element.29, f32[1,2,16,16]{2,3,0,1:T(8,128)S(1)} %get-tuple-element.28), kind=kOutput, calls=%fused_computation.4 | convolution fusion | flops 201327616 | bytes 4198400 | tf_op jit(solution)/shard_map/p...kb,pqbm->q...mk/dot_general | solution.py:65
  72.9 1.2 %copy.63 = f32[2,2,256,2,16,16]{2,5,4,3,1,0:T(8,128)S(1)} copy(f32[2,2,256,2,16,16]{2,4,5,3,1,0:T(8,128)S(1)} %fusion.3) | data formatting | bytes 4194304 | tf_op jit(solution)/shard_map/p...kb,pqbm->q...mk/transpose | solution.py:65
  74.2 0.3 copy.64
  74.8 1.0 convolution_bitcast_fusion.3
  76.2 1.6 %convolution_bitcast_fusion.2 = f32[2,256,2,16,16]{1,3,4,2,0:T(8,128)S(1)} fusion(f32[2,256,2,16,16]{1,3,4,2,0:T(8,128)S(1)} %pad_maximum_fusion.2, f32[1,2,16,16]{2,3,1,0:T(8,128)S(1)} %get-tuple-element.27, f32[1,2,16,16]{2,3,1,0:T(8,128)S(1)} %get-tuple-element.26), kind=kOutput, calls=%fused_computation.7 | convolution fusion | flops 100664320 | bytes 2101248 | tf_op jit(solution)/shard_map/p...kb,pqbm->q...mk/dot_general | solution.py:65
  77.8 0.3 copy.69
  78.7 1.3 %copy.71 = bf16[2,256,2,256]{1,2,0,3:T(2,128)(2,1)} copy(bf16[2,256,2,256]{1,3,2,0:T(8,128)(2,1)S(1)} %pad_maximum_fusion.3) | data formatting | bytes 1048576 | tf_op jit(solution)/shard_map/stack | solution.py:48
  80.1 6.8 %all-to-all-start.3 = ((bf16[2,256,2,256]{1,2,0,3:T(2,128)(2,1)}), bf16[2,256,2,256]{1,2,0,3:T(2,128)(2,1)S(1)}, u32[]{:S(2)}, u32[]{:S(2)}) async-start(bf16[2,256,2,256]{1,2,0,3:T(2,128)(2,1)} %copy.71), calls=%async_computation.3 | async-start | bytes 1048576 | tf_op jit(solution)/shard_map/all_to_all | solution.py:70
  87.0 14.4 %all-to-all-done.3 = bf16[2,256,2,256]{1,2,0,3:T(2,128)(2,1)S(1)} async-done(((bf16[2,256,2,256]{1,2,0,3:T(2,128)(2,1)}), bf16[2,256,2,256]{1,2,0,3:T(2,128)(2,1)S(1)}, u32[]{:S(2)}, u32[]{:S(2)}) %all-to-all-start.3) | async-done | bytes 524320 | tf_op jit(solution)/shard_map/all_to_all | solution.py:70
  101.4 0.5 copy.73
  102.2 0.4 fusion.7
  102.6 0.7 copy.74
  103.3 4.1 %all-to-all-start.4 = ((bf16[1,256,16,16]{1,3,0,2:T(8,128)(2,1)}), bf16[1,256,16,16]{1,3,0,2:T(8,128)(2,1)S(1)}, u32[]{:S(2)}, u32[]{:S(2)}) async-start(bf16[1,256,16,16]{1,3,0,2:T(8,128)(2,1)} %copy.74), calls=%async_computation.4 | async-start | bytes 262144 | tf_op jit(solution)/shard_map/all_to_all | solution.py:76
  107.4 7.9 %all-to-all-done.4 = bf16[1,256,16,16]{1,3,0,2:T(8,128)(2,1)S(1)} async-done(((bf16[1,256,16,16]{1,3,0,2:T(8,128)(2,1)}), bf16[1,256,16,16]{1,3,0,2:T(8,128)(2,1)S(1)}, u32[]{:S(2)}, u32[]{:S(2)}) %all-to-all-start.4) | async-done | bytes 131104 | tf_op jit(solution)/shard_map/all_to_all | solution.py:76
  115.4 0.8 copy.76
  (45 shorter events, 3.4 us)
Async XLA Ops:
  0.0 16.8 %copy-start = (f32[256,256]{1,0:T(8,128)S(1)}, f32[256,256]{1,0:T(8,128)}, u32[]{:S(2)}) copy-start(f32[256,256]{1,0:T(8,128)} %param.6) | copy-start | bytes 786436
  2.2 13.0 %all-to-all-start = ((bf16[3,512,128]{2,0,1:T(4,128)(2,1)}), bf16[3,512,128]{2,0,1:T(4,128)(2,1)S(1)}, u32[]{:S(2)}, u32[]{:S(2)}) async-start(bf16[3,512,128]{2,0,1:T(4,128)(2,1)} %copy.50), calls=%async_computation | async-start | bytes 1048576 | tf_op jit(solution)/shard_map/all_to_all | solution.py:120
  15.4 2.1 %collective-permute-start = (bf16[3,256,6]{1,2,0:T(8,128)(2,1)S(1)}, bf16[3,256,6]{1,2,0:T(8,128)(2,1)S(1)}, u32[]{:S(2)}, u32[]{:S(2)}) collective-permute-start(bf16[3,256,6]{1,2,0:T(8,128)(2,1)S(1)} %slice.149), channel_id=1, source_target_pairs={{0,2},{2,4},{4,6},{6,8},{8,10},{10,12},{12,14},{14,16},{16,18},{18... | collective-permute-start | bytes 27656 | tf_op jit(solution)/shard_map/ppermute | solution.py:12
  19.3 19.1 %all-to-all-start.1 = ((bf16[2,256,1,256]{1,0,2,3:T(2,128)(2,1)}), bf16[2,256,1,256]{1,0,2,3:T(2,128)(2,1)S(1)}, u32[]{:S(2)}, u32[]{:S(2)}) async-start(bf16[2,256,1,256]{1,0,2,3:T(2,128)(2,1)} %copy.55), calls=%async_computation.1 | async-start | bytes 524288 | tf_op jit(solution)/shard_map/all_to_all | solution.py:70
  41.4 26.6 %all-to-all-start.2 = ((bf16[4,256,32,16]{1,3,0,2:T(8,128)(2,1)}), bf16[4,256,32,16]{1,3,0,2:T(8,128)(2,1)S(1)}, u32[]{:S(2)}, u32[]{:S(2)}) async-start(bf16[4,256,32,16]{1,3,0,2:T(8,128)(2,1)} %copy.58), calls=%async_computation.2 | async-start | bytes 2097152 | tf_op jit(solution)/shard_map/all_to_all | solution.py:76
  80.1 21.3 %all-to-all-start.3 = ((bf16[2,256,2,256]{1,2,0,3:T(2,128)(2,1)}), bf16[2,256,2,256]{1,2,0,3:T(2,128)(2,1)S(1)}, u32[]{:S(2)}, u32[]{:S(2)}) async-start(bf16[2,256,2,256]{1,2,0,3:T(2,128)(2,1)} %copy.71), calls=%async_computation.3 | async-start | bytes 1048576 | tf_op jit(solution)/shard_map/all_to_all | solution.py:70
  101.4 13.9 %copy-start.1 = (f32[256]{0:T(256)S(1)}, f32[256]{0:T(256)}, u32[]{:S(2)}) copy-start(f32[256]{0:T(256)} %param.7) | copy-start | bytes 3076
  103.3 12.0 %all-to-all-start.4 = ((bf16[1,256,16,16]{1,3,0,2:T(8,128)(2,1)}), bf16[1,256,16,16]{1,3,0,2:T(8,128)(2,1)S(1)}, u32[]{:S(2)}, u32[]{:S(2)}) async-start(bf16[1,256,16,16]{1,3,0,2:T(8,128)(2,1)} %copy.74), calls=%async_computation.4 | async-start | bytes 262144 | tf_op jit(solution)/shard_map/all_to_all | solution.py:76
where the time goes:
time: 117 us; the launch traced here: 116 us
  waiting for transfers between devices  62.4 us (53%)
  starting transfers between devices  29.3 us (25%)
  local copies, waits for them, and re-layouts  12.5 us (11%)
  matrix products  8.33 us (7%)
  other arithmetic  3.26 us (3%)
    all_to_all x2, waiting for transfers between devices, to_rows(): lax.all_to_all(values.astype(jnp.bfloat16), 'ctx', split_axis=2, concat_a...  30 us
    all_to_all x2, waiting for transfers between devices, to_columns(): lax.all_to_all(values.astype(jnp.bfloat16), 'ctx', split_axis=3, concat_a...  24.2 us
    all_to_all x2, starting transfers between devices, to_columns(): lax.all_to_all(values.astype(jnp.bfloat16), 'ctx', split_axis=3, concat_a...  15.8 us
    all_to_all x2, starting transfers between devices, to_rows(): lax.all_to_all(values.astype(jnp.bfloat16), 'ctx', split_axis=2, concat_a...  7.93 us
    all_to_all x1, waiting for transfers between devices, local(): grouped = lax.all_to_all(qkv, 'ch', split_axis=1, concat_axis=2, tiled=True)  7.48 us
    dot_general x2, matrix products, local_transform(): result = jnp.einsum('p...kb,pqbm->q...mk', part, inner, precision=highest)  4.59 us
    all_to_all x1, starting transfers between devices, local(): grouped = lax.all_to_all(qkv, 'ch', split_axis=1, concat_axis=2, tiled=True)  4.23 us
  transfers between devices with their start and end apart: 6, of which 6 were waited for; matrix products, arithmetic and copies ran while one was open for 2% of the time, Pallas kernels for 0%

commit v1 on v0

--- a/solution.py
+++ b/solution.py
@@ -1,9 +1,311 @@
+import functools
 import math
 
 import jax
 import jax.numpy as jnp
+import ml_dtypes
+import numpy as np
 from jax import lax
+from jax.experimental import pallas as pl
+from jax.experimental.pallas import tpu as pltpu
 from jax.sharding import PartitionSpec as P
+
+MESH = pl.DeviceIdType.MESH
+F32 = jnp.float32
+BF16 = jnp.bfloat16
+
+
+def tables(devices, width, chans):
+    total = 2 * devices * width
+    a = np.arange(devices)
+    k1 = np.arange(devices) + 0.5
+    eye = np.eye(chans)
+    angle = 2 * np.pi * np.outer(k1, a) / (2 * devices)
+    forward = np.concatenate([np.kron(np.cos(angle), eye), np.kron(-np.sin(angle), eye)], 0)
+    inverse = np.concatenate([np.kron(np.cos(angle.T), eye), np.kron(-np.sin(angle.T), eye)], 1)
+    inverse = inverse * (2.0 / total)
+    b = np.arange(width)
+    turn = 2 * np.pi * np.outer(k1, b) / total
+    twist = np.stack([np.cos(turn), np.sin(turn)])
+    inner = 2 * np.pi * (np.outer(b, b) % width) / width
+    cos, sin = np.cos(inner), np.sin(inner)
+    wide = np.stack(
+        [np.block([[cos, -sin], [sin, cos]]), np.block([[cos, sin], [-sin, cos]])]
+    )
+    low = lambda x: jnp.asarray(x.astype(ml_dtypes.bfloat16))
+    return (
+        low(forward),
+        low(inverse),
+        low(wide),
+        jnp.asarray(twist.astype(np.float32)[:, :, None, :]),
+    )
+
+
+def kernel(
+    lanes, groups, reach,
+    qkv, taps, filters, skip, fwd_hbm, inv_hbm, wide_hbm, twist_hbm,
+    out,
+    kvbuf, qbuf, fraw, fsend, fbuf, tapv, tapb, skipb, fwd, inv, wide, twist,
+    gbuf, hspec, vbuf, mbuf,
+    load_sem, own_sem, send_sem, recv_sem,
+):
+    devices = lanes * groups
+    chans = fbuf.shape[1]
+    width = fbuf.shape[2]
+    mine = lax.axis_index("ctx")
+    side = lax.axis_index("ch")
+    me = mine * groups + side
+    per_side = lanes * chans
+
+    def rows_of(i, j):
+        return pl.ds(pl.multiple_of(j * per_side + i * chans, chans), chans)
+
+    def side_rows(i):
+        return pl.ds(pl.multiple_of(i * chans, chans), chans)
+
+    load_f = pltpu.make_async_copy(filters, fraw, load_sem.at[0])
+    load_f.start()
+    own_rows = rows_of(mine, side)
+    loads = [
+        pltpu.make_async_copy(taps.at[:, own_rows], tapv, load_sem.at[1]),
+        pltpu.make_async_copy(fwd_hbm, fwd, load_sem.at[2]),
+        pltpu.make_async_copy(wide_hbm, wide, load_sem.at[3]),
+        pltpu.make_async_copy(twist_hbm, twist, load_sem.at[4]),
+        pltpu.make_async_copy(inv_hbm, inv, load_sem.at[5]),
+    ]
+    own_kv = pltpu.make_async_copy(
+        qkv.at[pl.ds(1, 2), own_rows], kvbuf.at[:, me + 1], own_sem.at[0]
+    )
+    own_q = pltpu.make_async_copy(qkv.at[0, own_rows], qbuf.at[me + 1], own_sem.at[1])
+    own_kv.start()
+    own_q.start()
+    for load in loads:
+        load.start()
+
+    barrier = pltpu.get_barrier_semaphore()
+
+    def greet(d, carry):
+        t = lax.rem(me + d, devices)
+        pl.semaphore_signal(
+            barrier, inc=1, device_id=(t // groups, t % groups), device_id_type=MESH
+        )
+        return carry
+
+    lax.fori_loop(1, devices, greet, 0)
+
+    kvbuf[0, 0] = jnp.zeros((chans, width), BF16)
+    kvbuf[1, 0] = jnp.zeros((chans, width), BF16)
+    qbuf[0] = jnp.zeros((chans, width), BF16)
+    load_f.wait()
+    for g in range(groups):
+        fsend[g] = fraw[:, g * width : (g + 1) * width].astype(BF16)
+
+    pl.semaphore_wait(barrier, devices - 1)
+
+    def send_filters(d, carry):
+        i = lax.rem(mine + d, lanes)
+        pltpu.make_async_remote_copy(
+            src_ref=fsend.at[:, side_rows(i)],
+            dst_ref=fbuf.at[pl.ds(mine * groups, groups)],
+            send_sem=send_sem.at[0], recv_sem=recv_sem.at[0],
+            device_id=(i, side), device_id_type=MESH,
+        ).start()
+        return carry
+
+    def send_kv(d, carry):
+        t = lax.rem(me + d, devices)
+        i, j = t // groups, t % groups
+        pltpu.make_async_remote_copy(
+            src_ref=qkv.at[pl.ds(1, 2), rows_of(i, j)],
+            dst_ref=kvbuf.at[:, me + 1],
+            send_sem=send_sem.at[1], recv_sem=recv_sem.at[1],
+            device_id=(i, j), device_id_type=MESH,
+        ).start()
+        return carry
+
+    def send_q(d, carry):
+        t = lax.rem(me + d, devices)
+        i, j = t // groups, t % groups
+        pltpu.make_async_remote_copy(
+            src_ref=qkv.at[0, rows_of(i, j)],
+            dst_ref=qbuf.at[me + 1],
+            send_sem=send_sem.at[2], recv_sem=recv_sem.at[2],
+            device_id=(i, j), device_id_type=MESH,
+        ).start()
+        return carry
+
+    lax.fori_loop(1, lanes, send_filters, 0)
+    lax.fori_loop(1, devices, send_kv, 0)
+    lax.fori_loop(1, devices, send_q, 0)
+    own_f = pltpu.make_async_copy(
+        fsend.at[:, side_rows(mine)], fbuf.at[pl.ds(mine * groups, groups)], own_sem.at[2]
+    )
+    own_f.start()
+
+    for load in loads:
+        load.wait()
+    for s in range(3):
+        for i in range(reach + 1):
+            tapb[s, i] = jnp.broadcast_to(tapv[s, :, i : i + 1], (chans, width))
+    pick = lax.broadcasted_iota(jnp.int32, (chans, per_side), 1) == (
+        mine * chans + lax.broadcasted_iota(jnp.int32, (chans, per_side), 0)
+    )
+    column = jnp.sum(jnp.where(pick, skip[...], 0.0), axis=1, keepdims=True)
+    skipb[...] = jnp.broadcast_to(column, (chans, width))
+
+    step = 8
+    block = step * chans
+    half = devices * chans
+
+    def dot(left, right):
+        return jnp.dot(left, right, preferred_element_type=F32)
+
+    def forward(signal, r0, k0):
+        real = dot(fwd[pl.ds(r0, block), :], signal).reshape(step, chans, width)
+        imag = dot(fwd[pl.ds(half + r0, block), :], signal).reshape(step, chans, width)
+        cos, sin = twist[0, pl.ds(k0, step)], twist[1, pl.ds(k0, step)]
+        turned = jnp.concatenate(
+            [
+                (real * cos + imag * sin).astype(BF16).reshape(block, width),
+                (imag * cos - real * sin).astype(BF16).reshape(block, width),
+            ],
+            axis=1,
+        )
+        return dot(turned, wide[0])
+
+    own_f.wait()
+    got_f = fbuf.at[pl.ds(0, devices - groups)]
+    pltpu.make_async_copy(got_f, got_f, recv_sem.at[0]).wait()
+
+    @pl.loop(0, devices // step)
+    def _(n):
+        r0 = pl.multiple_of(n * block, block)
+        hspec[pl.ds(r0, block), :] = forward(
+            fbuf[...].reshape(half, width), r0, n * step
+        )
+
+    own_kv.wait()
+    got_kv = kvbuf.at[:, pl.ds(0, devices - 1)]
+    pltpu.make_async_copy(got_kv, got_kv, recv_sem.at[1]).wait()
+    fstep = 4
+    lane = lax.broadcasted_iota(jnp.int32, (fstep * chans, width), 1)
+
+    def feature(stream, cur, prev):
+        cur = cur.astype(F32).reshape(fstep * chans, width)
+        prev = prev.astype(F32).reshape(fstep * chans, width)
+        acc = tapb[stream, 0] * cur.reshape(fstep, chans, width)
+        for i in range(1, reach + 1):
+            moved = pltpu.roll(jnp.where(lane >= width - i, prev, cur), i, 1)
+            acc = acc + tapb[stream, i] * moved.reshape(fstep, chans, width)
+        return acc
+
+    @pl.loop(0, devices // fstep)
+    def _(n):
+        a0 = n * fstep
+        key = feature(1, kvbuf[0, pl.ds(a0 + 1, fstep)], kvbuf[0, pl.ds(a0, fstep)])
+        value = feature(2, kvbuf[1, pl.ds(a0 + 1, fstep)], kvbuf[1, pl.ds(a0, fstep)])
+        gbuf[pl.ds(a0, fstep)] = (key * value).astype(BF16)
+
+    @pl.loop(0, devices // step)
+    def _(n):
+        r0 = pl.multiple_of(n * block, block)
+        spec = forward(gbuf[...].reshape(half, width), r0, n * step)
+        filt = hspec[pl.ds(r0, block), :]
+        sr, si = spec[:, :width], spec[:, width:]
+        fr, fi = filt[:, :width], filt[:, width:]
+        prod = jnp.concatenate(
+            [(sr * fr - si * fi).astype(BF16), (sr * fi + si * fr).astype(BF16)], axis=1
+        )
+        back = dot(prod, wide[1])
+        br = back[:, :width].reshape(step, chans, width)
+        bi = back[:, width:].reshape(step, chans, width)
+        cos, sin = twist[0, pl.ds(n * step, step)], twist[1, pl.ds(n * step, step)]
+        vbuf[pl.ds(r0, block), :] = (br * cos - bi * sin).astype(BF16).reshape(block, width)
+        vbuf[pl.ds(half + r0, block), :] = (
+            (br * sin + bi * cos).astype(BF16).reshape(block, width)
+        )
+
+    own_q.wait()
+    got_q = qbuf.at[pl.ds(0, devices - 1)]
+    pltpu.make_async_copy(got_q, got_q, recv_sem.at[2]).wait()
+
+    @pl.loop(0, devices // fstep)
+    def _(n):
+        a0 = n * fstep
+        rows = pl.ds(pl.multiple_of(a0 * chans, fstep * chans), fstep * chans)
+        query = feature(0, qbuf[pl.ds(a0 + 1, fstep)], qbuf[pl.ds(a0, fstep)])
+        query = query.astype(BF16).astype(F32)
+        conv = dot(inv[rows, :], vbuf[...]).reshape(fstep, chans, width)
+        signal = gbuf[pl.ds(a0, fstep)].astype(F32)
+        mbuf[pl.ds(a0, fstep)] = (query * (conv + skipb[...] * signal)).astype(BF16)
+
+    def send_out(d, carry):
+        i = lax.rem(mine + d, lanes)
+        pltpu.make_async_remote_copy(
+            src_ref=mbuf.at[pl.ds(i * groups, groups)],
+            dst_ref=out.at[:, side_rows(mine)],
+            send_sem=send_sem.at[3], recv_sem=recv_sem.at[3],
+            device_id=(i, side), device_id_type=MESH,
+        ).start()
+        return carry
+
+    lax.fori_loop(1, lanes, send_out, 0)
+    own_o = pltpu.make_async_copy(
+        mbuf.at[pl.ds(mine * groups, groups)], out.at[:, side_rows(mine)], own_sem.at[3]
+    )
+    own_o.start()
+
+    sent_f = fbuf.at[pl.ds(0, devices - groups)]
+    pltpu.make_async_copy(sent_f, sent_f, send_sem.at[0]).wait()
+    pltpu.make_async_copy(got_kv, got_kv, send_sem.at[1]).wait()
+    pltpu.make_async_copy(got_q, got_q, send_sem.at[2]).wait()
+    got_o = mbuf.at[pl.ds(0, devices - groups)]
+    pltpu.make_async_copy(got_o, got_o, send_sem.at[3]).wait()
+    own_o.wait()
+    pltpu.make_async_copy(got_o, got_o, recv_sem.at[3]).wait()
+
+
+def fused_local(lanes, groups, qkv, conv_taps, filters, skip):
+    devices = lanes * groups
+    channels, width = qkv.shape[1], qkv.shape[2]
+    chans = channels // devices
+    count = conv_taps.shape[2]
+    fwd, inv, wide, twist = tables(devices, width, chans)
+    any_spec = pl.BlockSpec(memory_space=pl.ANY)
+    vmem_spec = pl.BlockSpec(memory_space=pltpu.VMEM)
+    per_side = lanes * chans
+    landed = pl.pallas_call(
+        functools.partial(kernel, lanes, groups, count - 1),
+        out_shape=jax.ShapeDtypeStruct((groups, per_side, width), BF16),
+        in_specs=[any_spec, any_spec, any_spec, vmem_spec] + [any_spec] * 4,
+        out_specs=any_spec,
+        scratch_shapes=[
+            pltpu.VMEM((2, devices + 1, chans, width), BF16),
+            pltpu.VMEM((devices + 1, chans, width), BF16),
+            pltpu.VMEM(filters.shape, F32),
+            pltpu.VMEM((groups, per_side, width), BF16),
+            pltpu.VMEM((devices, chans, width), BF16),
+            pltpu.VMEM((3, chans, count), F32),
+            pltpu.VMEM((3, count, chans, width), F32),
+            pltpu.VMEM((chans, width), F32),
+            pltpu.VMEM(fwd.shape, BF16),
+            pltpu.VMEM(inv.shape, BF16),
+            pltpu.VMEM(wide.shape, BF16),
+            pltpu.VMEM(twist.shape, F32),
+            pltpu.VMEM((devices, chans, width), BF16),
+            pltpu.VMEM((channels, 2 * width), F32),
+            pltpu.VMEM((2 * channels, width), BF16),
+            pltpu.VMEM((devices, chans, width), BF16),
+            pltpu.SemaphoreType.DMA((6,)),
+            pltpu.SemaphoreType.DMA((4,)),
+            pltpu.SemaphoreType.DMA((4,)),
+            pltpu.SemaphoreType.DMA((4,)),
+        ],
+        compiler_params=pltpu.CompilerParams(
+            collective_id=0, has_side_effects=True, vmem_limit_bytes=32 * 1024 * 1024
+        ),
+    )(qkv, conv_taps, filters, skip.reshape(1, -1), fwd, inv, wide, twist)
+    return landed.transpose(1, 0, 2).reshape(per_side, groups * width)
 
 
 def from_behind(shard, axis, by):
@@ -129,8 +431,17 @@
 
 
 def solution(mesh):
+    lanes, groups = mesh.shape["ctx"], mesh.shape["ch"]
+
+    def body(qkv, conv_taps, filters, skip):
+        chans = qkv.shape[1] // (lanes * groups)
+        fits = chans % 16 == 0 and (lanes * groups) % 8 == 0 and qkv.shape[2] % 128 == 0
+        if fits:
+            return fused_local(lanes, groups, qkv, conv_taps, filters, skip)
+        return local(qkv, conv_taps, filters, skip)
+
     return jax.shard_map(
-        local,
+        body,
         mesh=mesh,
         in_specs=(P(None, None, ("ctx", "ch")), P(), P("ch", "ctx"), P("ch")),
         out_specs=P("ch", "ctx"),

time: 117 us -> 34 us (0.29)
  waiting for transfers between devices: 62.4 us -> 0 us
  starting transfers between devices: 29.3 us -> 0 us
  Pallas kernels: 0 us -> 28.3 us
  matrix products: 8.33 us -> 0 us
  local copies, waits for them, and re-layouts: 12.5 us -> 5.43 us
  other arithmetic: 3.26 us -> 0 us
    all_to_all x5 -> x0, waiting for transfers between devices: 61.7 us -> none  [the longest x2 30 us: to_rows(): lax.all_to_all(values.astype(jnp.bfloat16), 'ctx', split_axis=2, concat_a...]
    pallas_call x0 -> x1, Pallas kernels: none -> 28.3 us  [fused_local(): pl.pallas_call(functools.partial(kernel, lanes, groups, count - 1), out_s...]
    all_to_all x5 -> x0, starting transfers between devices: 28 us -> none  [the longest x2 15.8 us: to_columns(): lax.all_to_all(values.astype(jnp.bfloat16), 'ctx', split_axis=3, concat_a...]
    dot_general x6 -> x0, matrix products: 8.33 us -> none  [the longest x2 4.59 us: local_transform(): result = jnp.einsum('p...kb,pqbm->q...mk', part, inner, precision=highest)]
    convert_element_type x4 -> x0, local copies, waits for them, and re-layouts: 3.04 us -> none  [the longest x2 2.26 us: to_rows(): values.astype(jnp.bfloat16)]
    another operation x2 -> x0, local copies, waits for them, and re-layouts: 2.29 us -> none  [the longest x1 1.33 us: twisted(): jnp.stack([values[0] * cosine - values[1] * sine, values[0] * sine + valu...]
    unnamed x10 -> x15, local copies, waits for them, and re-layouts: 2.29 us -> 4.56 us
    slice x5 -> x0, local copies, waits for them, and re-layouts: 1.9 us -> none  [the longest x1 1.2 us: featurize(): taps[:, :, offset:offset + 1]]
  transfers between devices with their start and end apart: 6 -> 0, of which waited for: 6 -> 0; matrix products, arithmetic and copies ran while one was open for 2% -> 0% of each run, Pallas kernels for 0% -> 0%
where the time goes in v1:
time: 34 us; the launch traced here: 33.8 us
  Pallas kernels  28.3 us (83%)
  local copies, waits for them, and re-layouts  5.43 us (16%)
    pallas_call x1, Pallas kernels, fused_local(): pl.pallas_call(functools.partial(kernel, lanes, groups, count - 1), out_s...  28.3 us
    unnamed x15, local copies, waits for them, and re-layouts  4.56 us
    reshape x1, local copies, waits for them, and re-layouts, fused_local(): return landed.transpose(1, 0, 2).reshape(per_side, groups * width)  0.76 us

profile of v1, /device:TPU:0, one launch (start us, length us, event | category | flops | bytes accessed | tf_op | source)
XLA Modules:
  0.0 33.8 jit_solution(3759156849964608497)
XLA Ops:
  0.0 0.0 copy-start.2
  0.0 0.0 copy-start.3
  0.0 0.0 copy-start.5
  0.0 0.0 copy-start.6
  0.0 1.1 %copy.10.taps = f32[3,512,7]{2,1,0:T(8,128)S(1)} copy(f32[3,512,7]{1,2,0:T(8,128)} %param.9) | data formatting | bytes 86016 | tf_op args[1]
  1.2 0.0 copy-done.2
  1.2 0.0 copy-done.3
  1.2 0.0 copy-done.5
  1.2 0.0 copy-done.6
  1.2 0.0 copy-start
  1.2 1.2 %copy-done = bf16[512,1024]{1,0:T(8,128)(2,1)S(1)} copy-done((bf16[512,1024]{1,0:T(8,128)(2,1)S(1)}, bf16[512,1024]{1,0:T(8,128)(2,1)}, u32[]{:S(2)}) %copy-start) | copy-done | bytes 1048600
  2.4 0.0 copy-start.1
  2.4 1.2 %copy-done.1 = bf16[1024,512]{1,0:T(8,128)(2,1)S(1)} copy-done((bf16[1024,512]{1,0:T(8,128)(2,1)S(1)}, bf16[1024,512]{1,0:T(8,128)(2,1)}, u32[]{:S(2)}) %copy-start.1) | copy-done | bytes 1048600
  3.7 0.0 copy-start.4
  3.7 0.9 %copy-done.4 = bf16[2,256,256]{2,1,0:T(8,128)(2,1)S(1)} copy-done((bf16[2,256,256]{2,1,0:T(8,128)(2,1)S(1)}, bf16[2,256,256]{2,1,0:T(8,128)(2,1)}, u32[]{:S(2)}) %copy-start.4) | copy-done | bytes 262168
  4.6 28.3 %shard_map.82 = bf16[2,256,128]{2,1,0:T(8,128)(2,1)S(1)} custom-call(bf16[3,512,128]{2,1,0:T(8,128)(2,1)S(1)} %copy-done.2, f32[3,512,7]{2,1,0:T(8,128)S(1)} %copy.10.taps, f32[256,256]{1,0:T(8,128)S(1)} %copy-done.3, f32[1,256]{1,0:T(1,128)S(1)} %bitcast.4, bf16[1024,512]{1,0:T(8,128)(2,1)S(1)} %copy-done.1, bf16[512,1024]{1,0:T(8,128)(2,1)S(1)} %copy-done, ...), custom_call_target="tpu_custom_call" | custom-call | tf_op jit(solution)/shard_map/pallas_call | solution.py:277
  32.9 0.1 copy.11
  33.1 0.8 %copy.12 = bf16[256,256]{1,0:T(8,128)(2,1)} copy(bf16[256,256]{0,1:T(8,128)(2,1)S(1)} %bitcast.5) | data formatting | bytes 262144 | tf_op jit(solution)/shard_map/reshape | solution.py:308
Async XLA Ops:
  0.0 1.2 %copy-start.2 = (bf16[3,512,128]{2,1,0:T(8,128)(2,1)S(1)}, bf16[3,512,128]{2,1,0:T(8,128)(2,1)}, u32[]{:S(2)}) copy-start(bf16[3,512,128]{2,1,0:T(8,128)(2,1)} %qkv.1) | copy-start | bytes 1179652
  0.0 1.2 %copy-start.3 = (f32[256,256]{1,0:T(8,128)S(1)}, f32[256,256]{1,0:T(8,128)}, u32[]{:S(2)}) copy-start(f32[256,256]{1,0:T(8,128)} %filters.1) | copy-start | bytes 786436
  0.0 1.2 %copy-start.5 = (f32[2,32,1,128]{3,2,1,0:T(1,128)S(1)}, f32[2,32,1,128]{3,2,1,0:T(1,128)}, u32[]{:S(2)}) copy-start(f32[2,32,1,128]{3,2,1,0:T(1,128)} %constant.11.clone.twist_hbm) | copy-start | bytes 98308
  0.0 1.2 %copy-start.6 = (f32[256]{0:T(256)S(1)}, f32[256]{0:T(256)}, u32[]{:S(2)}) copy-start(f32[256]{0:T(256)} %param.11) | copy-start | bytes 3076
  1.2 1.2 %copy-start = (bf16[512,1024]{1,0:T(8,128)(2,1)S(1)}, bf16[512,1024]{1,0:T(8,128)(2,1)}, u32[]{:S(2)}) copy-start(bf16[512,1024]{1,0:T(8,128)(2,1)} %constant.9.clone.inv_hbm) | copy-start | bytes 3145732
  2.4 1.2 %copy-start.1 = (bf16[1024,512]{1,0:T(8,128)(2,1)S(1)}, bf16[1024,512]{1,0:T(8,128)(2,1)}, u32[]{:S(2)}) copy-start(bf16[1024,512]{1,0:T(8,128)(2,1)} %constant.8.clone.fwd_hbm) | copy-start | bytes 3145732
  3.7 0.9 %copy-start.4 = (bf16[2,256,256]{2,1,0:T(8,128)(2,1)S(1)}, bf16[2,256,256]{2,1,0:T(8,128)(2,1)}, u32[]{:S(2)}) copy-start(bf16[2,256,256]{2,1,0:T(8,128)(2,1)} %constant.10.clone.wide_hbm) | copy-start | bytes 786436

commit v2 on v1

--- a/solution.py
+++ b/solution.py
@@ -45,40 +45,31 @@
     lanes, groups, reach,
     qkv, taps, filters, skip, fwd_hbm, inv_hbm, wide_hbm, twist_hbm,
     out,
-    kvbuf, qbuf, fraw, fsend, fbuf, tapv, tapb, skipb, fwd, inv, wide, twist,
-    gbuf, hspec, vbuf, mbuf,
+    qin, fraw, tapv, fwd, inv, wide, twist,
+    halo_out, halo_in, tapc, tapb, skipb,
+    fsend, fbuf, gsend, gbuf, qland, hspec, vbuf, mbuf, landed,
     load_sem, own_sem, send_sem, recv_sem,
 ):
     devices = lanes * groups
-    chans = fbuf.shape[1]
-    width = fbuf.shape[2]
+    chans, width = fbuf.shape[1], fbuf.shape[2]
+    channels = qin.shape[1]
     mine = lax.axis_index("ctx")
     side = lax.axis_index("ch")
     me = mine * groups + side
     per_side = lanes * chans
 
-    def rows_of(i, j):
-        return pl.ds(pl.multiple_of(j * per_side + i * chans, chans), chans)
-
     def side_rows(i):
         return pl.ds(pl.multiple_of(i * chans, chans), chans)
 
-    load_f = pltpu.make_async_copy(filters, fraw, load_sem.at[0])
-    load_f.start()
-    own_rows = rows_of(mine, side)
     loads = [
-        pltpu.make_async_copy(taps.at[:, own_rows], tapv, load_sem.at[1]),
-        pltpu.make_async_copy(fwd_hbm, fwd, load_sem.at[2]),
-        pltpu.make_async_copy(wide_hbm, wide, load_sem.at[3]),
-        pltpu.make_async_copy(twist_hbm, twist, load_sem.at[4]),
-        pltpu.make_async_copy(inv_hbm, inv, load_sem.at[5]),
+        pltpu.make_async_copy(src, dst, load_sem.at[n])
+        for n, (src, dst) in enumerate(
+            [
+                (qkv, qin), (filters, fraw), (taps, tapv), (fwd_hbm, fwd),
+                (wide_hbm, wide), (twist_hbm, twist), (inv_hbm, inv),
+            ]
+        )
     ]
-    own_kv = pltpu.make_async_copy(
-        qkv.at[pl.ds(1, 2), own_rows], kvbuf.at[:, me + 1], own_sem.at[0]
-    )
-    own_q = pltpu.make_async_copy(qkv.at[0, own_rows], qbuf.at[me + 1], own_sem.at[1])
-    own_kv.start()
-    own_q.start()
     for load in loads:
         load.start()
 
@@ -93,65 +84,137 @@
 
     lax.fori_loop(1, devices, greet, 0)
 
-    kvbuf[0, 0] = jnp.zeros((chans, width), BF16)
-    kvbuf[1, 0] = jnp.zeros((chans, width), BF16)
-    qbuf[0] = jnp.zeros((chans, width), BF16)
-    load_f.wait()
+    keep = 8
+    parts = width // keep
+    prows = channels // parts
+    lane = lax.broadcasted_iota(jnp.int32, (prows, width), 1)
+    loads[0].wait()
+    for s in range(3):
+        packed = jnp.zeros((prows, width), F32)
+        for g in range(parts):
+            rows = qin[s, g * prows : (g + 1) * prows].astype(F32)
+            moved = pltpu.roll(rows, (keep * (g + 1)) % width, 1)
+            packed = jnp.where((lane >= keep * g) & (lane < keep * (g + 1)), moved, packed)
+        halo_out[s] = packed.astype(BF16)
+    loads[1].wait()
     for g in range(groups):
         fsend[g] = fraw[:, g * width : (g + 1) * width].astype(BF16)
 
     pl.semaphore_wait(barrier, devices - 1)
+
+    after, before = me + 1, me - 1
+
+    def halo_copy(t):
+        return pltpu.make_async_remote_copy(
+            src_ref=halo_out, dst_ref=halo_in,
+            send_sem=send_sem.at[0], recv_sem=recv_sem.at[0],
+            device_id=(t // groups, t % groups), device_id_type=MESH,
+        )
+
+    @pl.when(me < devices - 1)
+    def _():
+        halo_copy(after).start()
 
     def send_filters(d, carry):
         i = lax.rem(mine + d, lanes)
         pltpu.make_async_remote_copy(
             src_ref=fsend.at[:, side_rows(i)],
             dst_ref=fbuf.at[pl.ds(mine * groups, groups)],
-            send_sem=send_sem.at[0], recv_sem=recv_sem.at[0],
+            send_sem=send_sem.at[1], recv_sem=recv_sem.at[1],
             device_id=(i, side), device_id_type=MESH,
         ).start()
         return carry
 
-    def send_kv(d, carry):
-        t = lax.rem(me + d, devices)
-        i, j = t // groups, t % groups
+    lax.fori_loop(1, lanes, send_filters, 0)
+    own_f = pltpu.make_async_copy(
+        fsend.at[:, side_rows(mine)], fbuf.at[pl.ds(mine * groups, groups)], own_sem.at[0]
+    )
+    own_f.start()
+
+    loads[2].wait()
+    for s in range(3):
+        wide_taps = jnp.concatenate(
+            [tapv[s], jnp.zeros((width - reach - 1, channels), F32)], axis=0
+        )
+        tapc[s] = wide_taps.T
+
+    @pl.loop(0, parts)
+    def _(g):
+        rows = pl.ds(pl.multiple_of(g * prows, prows), prows)
+        for s in range(3):
+            columns = tapc[s, rows]
+            for i in range(reach + 1):
+                tapb[s, i, rows] = jnp.broadcast_to(columns[:, i : i + 1], (prows, width))
+
+    pick = lax.broadcasted_iota(jnp.int32, (chans, per_side), 1) == (
+        mine * chans + lax.broadcasted_iota(jnp.int32, (chans, per_side), 0)
+    )
+    column = jnp.sum(jnp.where(pick, skip[...], 0.0), axis=1, keepdims=True)
+    skipb[...] = jnp.broadcast_to(column, (chans, width))
+
+    @pl.when(me > 0)
+    def _():
+        halo_copy(before).wait_recv()
+
+    @pl.when(me == 0)
+    def _():
+        halo_in[...] = jnp.zeros_like(halo_in)
+
+    def feature(stream, g):
+        rows = pl.ds(pl.multiple_of(g * prows, prows), prows)
+        cur = qin[stream, rows].astype(F32)
+        prev = pltpu.roll(halo_in[stream].astype(F32), width - keep - keep * g, 1)
+        acc = tapb[stream, 0, rows] * cur
+        for i in range(1, reach + 1):
+            moved = pltpu.roll(jnp.where(lane >= width - i, prev, cur), i, 1)
+            acc = acc + tapb[stream, i, rows] * moved
+        return acc
+
+    fold = prows // chans
+    side_parts = per_side // prows
+
+    @pl.loop(0, parts)
+    def _(n):
+        g = lax.rem(n + me // fold, parts)
+        gate = (feature(1, g) * feature(2, g)).astype(BF16)
+        gsend[pl.ds(pl.multiple_of(g * prows, prows), prows)] = gate
+        j = g // side_parts
+        for f in range(fold):
+            i = (g % side_parts) * fold + f
+            src = gsend.at[pl.ds(pl.multiple_of(g * prows + f * chans, chans), chans)]
+            own = jnp.logical_and(i == mine, j == side)
+
+            @pl.when(own)
+            def _():
+                pltpu.make_async_copy(src, gbuf.at[me], own_sem.at[1]).start()
+
+            @pl.when(jnp.logical_not(own))
+            def _():
+                pltpu.make_async_remote_copy(
+                    src_ref=src, dst_ref=gbuf.at[me],
+                    send_sem=send_sem.at[2], recv_sem=recv_sem.at[2],
+                    device_id=(i, j), device_id_type=MESH,
+                ).start()
+
+    for j in range(groups):
+
+        @pl.loop(0, side_parts)
+        def _(n):
+            rows = pl.ds(pl.multiple_of(n * prows, prows), prows)
+            mbuf[j, rows] = feature(0, j * side_parts + n).astype(BF16)
+
+    def send_query(d, carry):
+        j = lax.rem(side + d, groups)
         pltpu.make_async_remote_copy(
-            src_ref=qkv.at[pl.ds(1, 2), rows_of(i, j)],
-            dst_ref=kvbuf.at[:, me + 1],
-            send_sem=send_sem.at[1], recv_sem=recv_sem.at[1],
-            device_id=(i, j), device_id_type=MESH,
+            src_ref=mbuf.at[j], dst_ref=qland.at[side],
+            send_sem=send_sem.at[3], recv_sem=recv_sem.at[3],
+            device_id=(mine, j), device_id_type=MESH,
         ).start()
         return carry
 
-    def send_q(d, carry):
-        t = lax.rem(me + d, devices)
-        i, j = t // groups, t % groups
-        pltpu.make_async_remote_copy(
-            src_ref=qkv.at[0, rows_of(i, j)],
-            dst_ref=qbuf.at[me + 1],
-            send_sem=send_sem.at[2], recv_sem=recv_sem.at[2],
-            device_id=(i, j), device_id_type=MESH,
-        ).start()
-        return carry
-
-    lax.fori_loop(1, lanes, send_filters, 0)
-    lax.fori_loop(1, devices, send_kv, 0)
-    lax.fori_loop(1, devices, send_q, 0)
-    own_f = pltpu.make_async_copy(
-        fsend.at[:, side_rows(mine)], fbuf.at[pl.ds(mine * groups, groups)], own_sem.at[2]
-    )
-    own_f.start()
-
-    for load in loads:
-        load.wait()
-    for s in range(3):
-        for i in range(reach + 1):
-            tapb[s, i] = jnp.broadcast_to(tapv[s, :, i : i + 1], (chans, width))
-    pick = lax.broadcasted_iota(jnp.int32, (chans, per_side), 1) == (
-        mine * chans + lax.broadcasted_iota(jnp.int32, (chans, per_side), 0)
-    )
-    column = jnp.sum(jnp.where(pick, skip[...], 0.0), axis=1, keepdims=True)
-    skipb[...] = jnp.broadcast_to(column, (chans, width))
+    lax.fori_loop(1, groups, send_query, 0)
+    own_q = pltpu.make_async_copy(mbuf.at[side], qland.at[side], own_sem.at[2])
+    own_q.start()
 
     step = 8
     block = step * chans
@@ -173,38 +236,20 @@
         )
         return dot(turned, wide[0])
 
+    for load in loads[3:]:
+        load.wait()
     own_f.wait()
     got_f = fbuf.at[pl.ds(0, devices - groups)]
-    pltpu.make_async_copy(got_f, got_f, recv_sem.at[0]).wait()
+    pltpu.make_async_copy(got_f, got_f, recv_sem.at[1]).wait()
 
     @pl.loop(0, devices // step)
     def _(n):
         r0 = pl.multiple_of(n * block, block)
-        hspec[pl.ds(r0, block), :] = forward(
-            fbuf[...].reshape(half, width), r0, n * step
-        )
-
-    own_kv.wait()
-    got_kv = kvbuf.at[:, pl.ds(0, devices - 1)]
-    pltpu.make_async_copy(got_kv, got_kv, recv_sem.at[1]).wait()
-    fstep = 4
-    lane = lax.broadcasted_iota(jnp.int32, (fstep * chans, width), 1)
-
-    def feature(stream, cur, prev):
-        cur = cur.astype(F32).reshape(fstep * chans, width)
-        prev = prev.astype(F32).reshape(fstep * chans, width)
-        acc = tapb[stream, 0] * cur.reshape(fstep, chans, width)
-        for i in range(1, reach + 1):
-            moved = pltpu.roll(jnp.where(lane >= width - i, prev, cur), i, 1)
-            acc = acc + tapb[stream, i] * moved.reshape(fstep, chans, width)
-        return acc
-
-    @pl.loop(0, devices // fstep)
-    def _(n):
-        a0 = n * fstep
-        key = feature(1, kvbuf[0, pl.ds(a0 + 1, fstep)], kvbuf[0, pl.ds(a0, fstep)])
-        value = feature(2, kvbuf[1, pl.ds(a0 + 1, fstep)], kvbuf[1, pl.ds(a0, fstep)])
-        gbuf[pl.ds(a0, fstep)] = (key * value).astype(BF16)
+        hspec[pl.ds(r0, block), :] = forward(fbuf[...].reshape(half, width), r0, n * step)
+
+    gated = gbuf.at[pl.ds(0, devices - 1)]
+    pltpu.make_async_copy(gsend.at[pl.ds(0, chans)], gbuf.at[me], own_sem.at[1]).wait()
+    pltpu.make_async_copy(gated, gated, recv_sem.at[2]).wait()
 
     @pl.loop(0, devices // step)
     def _(n):
@@ -225,44 +270,57 @@
             (br * sin + bi * cos).astype(BF16).reshape(block, width)
         )
 
-    own_q.wait()
-    got_q = qbuf.at[pl.ds(0, devices - 1)]
-    pltpu.make_async_copy(got_q, got_q, recv_sem.at[2]).wait()
-
-    @pl.loop(0, devices // fstep)
+    fstep = 4
+    pieces = devices // fstep
+    ahead = fstep // groups
+
+    @pl.loop(0, pieces)
     def _(n):
-        a0 = n * fstep
+        m = lax.rem(n + mine // ahead, pieces)
+        a0 = m * fstep
         rows = pl.ds(pl.multiple_of(a0 * chans, fstep * chans), fstep * chans)
-        query = feature(0, qbuf[pl.ds(a0 + 1, fstep)], qbuf[pl.ds(a0, fstep)])
-        query = query.astype(BF16).astype(F32)
         conv = dot(inv[rows, :], vbuf[...]).reshape(fstep, chans, width)
         signal = gbuf[pl.ds(a0, fstep)].astype(F32)
-        mbuf[pl.ds(a0, fstep)] = (query * (conv + skipb[...] * signal)).astype(BF16)
-
-    def send_out(d, carry):
-        i = lax.rem(mine + d, lanes)
-        pltpu.make_async_remote_copy(
-            src_ref=mbuf.at[pl.ds(i * groups, groups)],
-            dst_ref=out.at[:, side_rows(mine)],
-            send_sem=send_sem.at[3], recv_sem=recv_sem.at[3],
-            device_id=(i, side), device_id_type=MESH,
-        ).start()
-        return carry
-
-    lax.fori_loop(1, lanes, send_out, 0)
-    own_o = pltpu.make_async_copy(
-        mbuf.at[pl.ds(mine * groups, groups)], out.at[:, side_rows(mine)], own_sem.at[3]
-    )
-    own_o.start()
+        gsend2 = (conv + skipb[...] * signal).astype(BF16)
+        fbuf[pl.ds(a0, fstep)] = gsend2
+        for f in range(ahead):
+            i = m * ahead + f
+            src = fbuf.at[pl.ds(i * groups, groups)]
+
+            @pl.when(i == mine)
+            def _():
+                pltpu.make_async_copy(
+                    src, landed.at[:, side_rows(mine)], own_sem.at[3]
+                ).start()
+
+            @pl.when(i != mine)
+            def _():
+                pltpu.make_async_remote_copy(
+                    src_ref=src, dst_ref=landed.at[:, side_rows(mine)],
+                    send_sem=send_sem.at[4], recv_sem=recv_sem.at[4],
+                    device_id=(i, side), device_id_type=MESH,
+                ).start()
+
+    @pl.when(me < devices - 1)
+    def _():
+        halo_copy(after).wait_send()
 
     sent_f = fbuf.at[pl.ds(0, devices - groups)]
-    pltpu.make_async_copy(sent_f, sent_f, send_sem.at[0]).wait()
-    pltpu.make_async_copy(got_kv, got_kv, send_sem.at[1]).wait()
-    pltpu.make_async_copy(got_q, got_q, send_sem.at[2]).wait()
-    got_o = mbuf.at[pl.ds(0, devices - groups)]
-    pltpu.make_async_copy(got_o, got_o, send_sem.at[3]).wait()
-    own_o.wait()
-    pltpu.make_async_copy(got_o, got_o, recv_sem.at[3]).wait()
+    pltpu.make_async_copy(sent_f, sent_f, send_sem.at[1]).wait()
+    pltpu.make_async_copy(gated, gated, send_sem.at[2]).wait()
+    others = qland.at[pl.ds(0, groups - 1)]
+    pltpu.make_async_copy(others, others, send_sem.at[3]).wait()
+    pltpu.make_async_copy(others, others, recv_sem.at[3]).wait()
+    own_q.wait()
+    pltpu.make_async_copy(sent_f, sent_f, send_sem.at[4]).wait()
+    pltpu.make_async_copy(
+        fbuf.at[pl.ds(0, groups)], landed.at[:, pl.ds(0, chans)], own_sem.at[3]
+    ).wait()
+    pltpu.make_async_copy(sent_f, sent_f, recv_sem.at[4]).wait()
+    for g in range(groups):
+        out[:, g * width : (g + 1) * width] = (
+            qland[g].astype(F32) * landed[g].astype(F32)
+        ).astype(BF16)
 
 
 def fused_local(lanes, groups, qkv, conv_taps, filters, skip):
@@ -271,41 +329,46 @@
     chans = channels // devices
     count = conv_taps.shape[2]
     fwd, inv, wide, twist = tables(devices, width, chans)
-    any_spec = pl.BlockSpec(memory_space=pl.ANY)
-    vmem_spec = pl.BlockSpec(memory_space=pltpu.VMEM)
+    hbm = pl.BlockSpec(memory_space=pltpu.HBM)
+    vmem = pl.BlockSpec(memory_space=pltpu.VMEM)
     per_side = lanes * chans
-    landed = pl.pallas_call(
+    halo = (3, channels * 8 // width, width)
+    return pl.pallas_call(
         functools.partial(kernel, lanes, groups, count - 1),
-        out_shape=jax.ShapeDtypeStruct((groups, per_side, width), BF16),
-        in_specs=[any_spec, any_spec, any_spec, vmem_spec] + [any_spec] * 4,
-        out_specs=any_spec,
+        out_shape=jax.ShapeDtypeStruct((per_side, groups * width), BF16),
+        in_specs=[hbm, hbm, hbm, vmem] + [hbm] * 4,
+        out_specs=vmem,
         scratch_shapes=[
-            pltpu.VMEM((2, devices + 1, chans, width), BF16),
-            pltpu.VMEM((devices + 1, chans, width), BF16),
+            pltpu.VMEM(qkv.shape, BF16),
             pltpu.VMEM(filters.shape, F32),
-            pltpu.VMEM((groups, per_side, width), BF16),
-            pltpu.VMEM((devices, chans, width), BF16),
-            pltpu.VMEM((3, chans, count), F32),
-            pltpu.VMEM((3, count, chans, width), F32),
-            pltpu.VMEM((chans, width), F32),
+            pltpu.VMEM((3, count, channels), F32),
             pltpu.VMEM(fwd.shape, BF16),
             pltpu.VMEM(inv.shape, BF16),
             pltpu.VMEM(wide.shape, BF16),
             pltpu.VMEM(twist.shape, F32),
+            pltpu.VMEM(halo, BF16),
+            pltpu.VMEM(halo, BF16),
+            pltpu.VMEM((3, channels, width), F32),
+            pltpu.VMEM((3, count, channels, width), F32),
+            pltpu.VMEM((chans, width), F32),
+            pltpu.VMEM((groups, per_side, width), BF16),
             pltpu.VMEM((devices, chans, width), BF16),
+            pltpu.VMEM((channels, width), BF16),
+            pltpu.VMEM((devices, chans, width), BF16),
+            pltpu.VMEM((groups, per_side, width), BF16),
             pltpu.VMEM((channels, 2 * width), F32),
             pltpu.VMEM((2 * channels, width), BF16),
-            pltpu.VMEM((devices, chans, width), BF16),
-            pltpu.SemaphoreType.DMA((6,)),
+            pltpu.VMEM((groups, per_side, width), BF16),
+            pltpu.VMEM((groups, per_side, width), BF16),
+            pltpu.SemaphoreType.DMA((7,)),
             pltpu.SemaphoreType.DMA((4,)),
-            pltpu.SemaphoreType.DMA((4,)),
-            pltpu.SemaphoreType.DMA((4,)),
+            pltpu.SemaphoreType.DMA((5,)),
+            pltpu.SemaphoreType.DMA((5,)),
         ],
         compiler_params=pltpu.CompilerParams(
-            collective_id=0, has_side_effects=True, vmem_limit_bytes=32 * 1024 * 1024
+            collective_id=0, has_side_effects=True, vmem_limit_bytes=60 * 1024 * 1024
         ),
-    )(qkv, conv_taps, filters, skip.reshape(1, -1), fwd, inv, wide, twist)
-    return landed.transpose(1, 0, 2).reshape(per_side, groups * width)
+    )(qkv, conv_taps.transpose(0, 2, 1), filters, skip.reshape(1, -1), fwd, inv, wide, twist)
 
 
 def from_behind(shard, axis, by):
@@ -435,7 +498,15 @@
 
     def body(qkv, conv_taps, filters, skip):
         chans = qkv.shape[1] // (lanes * groups)
-        fits = chans % 16 == 0 and (lanes * groups) % 8 == 0 and qkv.shape[2] % 128 == 0
+        fits = (
+            chans % 16 == 0
+            and qkv.shape[2] == 128
+            and (qkv.shape[1] // 16) % chans == 0
+            and (lanes * chans) % (qkv.shape[1] // 16) == 0
+            and (lanes * groups) % 8 == 0
+            and 4 % groups == 0
+            and conv_taps.shape[2] <= 8
+        )
         if fits:
             return fused_local(lanes, groups, qkv, conv_taps, filters, skip)
         return local(qkv, conv_taps, filters, skip)

time: 34 us -> 26.5 us (0.78)
  local copies, waits for them, and re-layouts: 5.43 us -> 1.57 us
  Pallas kernels: 28.3 us -> 24.8 us
    pallas_call x1, Pallas kernels: 28.3 us -> 24.8 us  [fused_local(): pl.pallas_call(functools.partial(kernel, lanes, groups, count - 1), out_s...]
    unnamed x15 -> x1, local copies, waits for them, and re-layouts: 4.56 us -> 1.57 us
    reshape x1 -> x0, local copies, waits for them, and re-layouts: 0.76 us -> none  [fused_local(): return landed.transpose(1, 0, 2).reshape(per_side, groups * width)]
where the time goes in v2:
time: 26.5 us; the launch traced here: 26.4 us
  Pallas kernels  24.8 us (94%)
  local copies, waits for them, and re-layouts  1.57 us (6%)
    pallas_call x1, Pallas kernels, fused_local(): pl.pallas_call(functools.partial(kernel, lanes, groups, count - 1), out_s...  24.8 us
    unnamed x1, local copies, waits for them, and re-layouts  1.57 us

profile of v2, /device:TPU:0, one launch (start us, length us, event | category | flops | bytes accessed | tf_op | source)
XLA Modules:
  0.0 26.4 jit_solution(7768402105501420233)
XLA Ops:
  0.0 24.8 %shard_map.82 = bf16[256,256]{1,0:T(8,128)(2,1)} custom-call(bf16[3,512,128]{2,1,0:T(8,128)(2,1)} %qkv.1, f32[3,7,512]{2,1,0:T(8,128)} %bitcast.2, f32[256,256]{1,0:T(8,128)} %filters.1, f32[1,256]{1,0:T(1,128)} %bitcast.3, bf16[1024,512]{1,0:T(8,128)(2,1)} %constant.8.clone.fwd_hbm, bf16[512,1024]{1,0:T(8,128)(2,1)} %constant.9.clone.inv_hbm, ...), custom_call_target="tpu_custom_call" | custom-call | tf_op jit(solution)/shard_map/pallas_call | solution.py:336
  24.8 1.6 %copy.10 = bf16[256,256]{1,0:T(8,128)(2,1)} copy(bf16[256,256]{1,0:T(8,128)(2,1)} %shard_map.82) | data formatting | bytes 262144

commit v3 on v2

--- a/solution.py
+++ b/solution.py
@@ -15,15 +15,13 @@
 BF16 = jnp.bfloat16
 
 
-def tables(devices, width, chans):
+def tables(devices, width):
     total = 2 * devices * width
     a = np.arange(devices)
     k1 = np.arange(devices) + 0.5
-    eye = np.eye(chans)
     angle = 2 * np.pi * np.outer(k1, a) / (2 * devices)
-    forward = np.concatenate([np.kron(np.cos(angle), eye), np.kron(-np.sin(angle), eye)], 0)
-    inverse = np.concatenate([np.kron(np.cos(angle.T), eye), np.kron(-np.sin(angle.T), eye)], 1)
-    inverse = inverse * (2.0 / total)
+    forward = np.concatenate([np.cos(angle), -np.sin(angle)], 0)
+    inverse = np.concatenate([np.cos(angle.T), -np.sin(angle.T)], 1) * (2.0 / total)
     b = np.arange(width)
     turn = 2 * np.pi * np.outer(k1, b) / total
     twist = np.stack([np.cos(turn), np.sin(turn)])
@@ -33,21 +31,16 @@
         [np.block([[cos, -sin], [sin, cos]]), np.block([[cos, sin], [-sin, cos]])]
     )
     low = lambda x: jnp.asarray(x.astype(ml_dtypes.bfloat16))
-    return (
-        low(forward),
-        low(inverse),
-        low(wide),
-        jnp.asarray(twist.astype(np.float32)[:, :, None, :]),
-    )
+    return low(forward), low(inverse), low(wide), jnp.asarray(twist.astype(np.float32))
 
 
 def kernel(
     lanes, groups, reach,
     qkv, taps, filters, skip, fwd_hbm, inv_hbm, wide_hbm, twist_hbm,
     out,
-    qin, fraw, tapv, fwd, inv, wide, twist,
+    qin, fraw, tapv, skipv, fwd, inv, wide, twist,
     halo_out, halo_in, tapc, tapb, skipb,
-    fsend, fbuf, gsend, gbuf, qland, hspec, vbuf, mbuf, landed,
+    fsend, fbuf, gsend, gbuf, qland, hspec, spread, mbuf, landed,
     load_sem, own_sem, send_sem, recv_sem,
 ):
     devices = lanes * groups
@@ -65,7 +58,7 @@
         pltpu.make_async_copy(src, dst, load_sem.at[n])
         for n, (src, dst) in enumerate(
             [
-                (qkv, qin), (filters, fraw), (taps, tapv), (fwd_hbm, fwd),
+                (qkv, qin), (filters, fraw), (taps, tapv), (skip, skipv), (fwd_hbm, fwd),
                 (wide_hbm, wide), (twist_hbm, twist), (inv_hbm, inv),
             ]
         )
@@ -149,7 +142,8 @@
     pick = lax.broadcasted_iota(jnp.int32, (chans, per_side), 1) == (
         mine * chans + lax.broadcasted_iota(jnp.int32, (chans, per_side), 0)
     )
-    column = jnp.sum(jnp.where(pick, skip[...], 0.0), axis=1, keepdims=True)
+    loads[3].wait()
+    column = jnp.sum(jnp.where(pick, skipv[...], 0.0), axis=1, keepdims=True)
     skipb[...] = jnp.broadcast_to(column, (chans, width))
 
     @pl.when(me > 0)
@@ -216,90 +210,91 @@
     own_q = pltpu.make_async_copy(mbuf.at[side], qland.at[side], own_sem.at[2])
     own_q.start()
 
-    step = 8
-    block = step * chans
     half = devices * chans
 
     def dot(left, right):
         return jnp.dot(left, right, preferred_element_type=F32)
 
-    def forward(signal, r0, k0):
-        real = dot(fwd[pl.ds(r0, block), :], signal).reshape(step, chans, width)
-        imag = dot(fwd[pl.ds(half + r0, block), :], signal).reshape(step, chans, width)
-        cos, sin = twist[0, pl.ds(k0, step)], twist[1, pl.ds(k0, step)]
-        turned = jnp.concatenate(
+    def part(value, c):
+        return value[:, c * width : (c + 1) * width]
+
+    def forward(source):
+        spread[...] = source[...].astype(F32).reshape(half, width)
+        columns = jnp.concatenate(
             [
-                (real * cos + imag * sin).astype(BF16).reshape(block, width),
-                (imag * cos - real * sin).astype(BF16).reshape(block, width),
+                spread[pl.ds(c, devices, stride=chans), :].astype(BF16)
+                for c in range(chans)
             ],
             axis=1,
         )
-        return dot(turned, wide[0])
-
-    for load in loads[3:]:
+        first = dot(fwd[...], columns)
+        cos, sin = twist[0], twist[1]
+        rows = []
+        for c in range(chans):
+            real, imag = part(first[:devices], c), part(first[devices:], c)
+            rows.append(
+                jnp.concatenate(
+                    [
+                        (real * cos + imag * sin).astype(BF16),
+                        (imag * cos - real * sin).astype(BF16),
+                    ],
+                    axis=1,
+                )
+            )
+        return dot(jnp.concatenate(rows, axis=0), wide[0])
+
+    for load in loads[4:]:
         load.wait()
     own_f.wait()
     got_f = fbuf.at[pl.ds(0, devices - groups)]
     pltpu.make_async_copy(got_f, got_f, recv_sem.at[1]).wait()
-
-    @pl.loop(0, devices // step)
-    def _(n):
-        r0 = pl.multiple_of(n * block, block)
-        hspec[pl.ds(r0, block), :] = forward(fbuf[...].reshape(half, width), r0, n * step)
+    hspec[...] = forward(fbuf)
 
     gated = gbuf.at[pl.ds(0, devices - 1)]
     pltpu.make_async_copy(gsend.at[pl.ds(0, chans)], gbuf.at[me], own_sem.at[1]).wait()
     pltpu.make_async_copy(gated, gated, recv_sem.at[2]).wait()
 
-    @pl.loop(0, devices // step)
-    def _(n):
-        r0 = pl.multiple_of(n * block, block)
-        spec = forward(gbuf[...].reshape(half, width), r0, n * step)
-        filt = hspec[pl.ds(r0, block), :]
-        sr, si = spec[:, :width], spec[:, width:]
-        fr, fi = filt[:, :width], filt[:, width:]
-        prod = jnp.concatenate(
-            [(sr * fr - si * fi).astype(BF16), (sr * fi + si * fr).astype(BF16)], axis=1
-        )
-        back = dot(prod, wide[1])
-        br = back[:, :width].reshape(step, chans, width)
-        bi = back[:, width:].reshape(step, chans, width)
-        cos, sin = twist[0, pl.ds(n * step, step)], twist[1, pl.ds(n * step, step)]
-        vbuf[pl.ds(r0, block), :] = (br * cos - bi * sin).astype(BF16).reshape(block, width)
-        vbuf[pl.ds(half + r0, block), :] = (
-            (br * sin + bi * cos).astype(BF16).reshape(block, width)
-        )
-
-    fstep = 4
-    pieces = devices // fstep
-    ahead = fstep // groups
-
-    @pl.loop(0, pieces)
-    def _(n):
-        m = lax.rem(n + mine // ahead, pieces)
-        a0 = m * fstep
-        rows = pl.ds(pl.multiple_of(a0 * chans, fstep * chans), fstep * chans)
-        conv = dot(inv[rows, :], vbuf[...]).reshape(fstep, chans, width)
-        signal = gbuf[pl.ds(a0, fstep)].astype(F32)
-        gsend2 = (conv + skipb[...] * signal).astype(BF16)
-        fbuf[pl.ds(a0, fstep)] = gsend2
-        for f in range(ahead):
-            i = m * ahead + f
-            src = fbuf.at[pl.ds(i * groups, groups)]
-
-            @pl.when(i == mine)
-            def _():
-                pltpu.make_async_copy(
-                    src, landed.at[:, side_rows(mine)], own_sem.at[3]
-                ).start()
-
-            @pl.when(i != mine)
-            def _():
-                pltpu.make_async_remote_copy(
-                    src_ref=src, dst_ref=landed.at[:, side_rows(mine)],
-                    send_sem=send_sem.at[4], recv_sem=recv_sem.at[4],
-                    device_id=(i, side), device_id_type=MESH,
-                ).start()
+    spec = forward(gbuf)
+    sr, si = part(spec, 0), part(spec, 1)
+    fr, fi = hspec[:, :width], hspec[:, width:]
+    prod = jnp.concatenate(
+        [(sr * fr - si * fi).astype(BF16), (sr * fi + si * fr).astype(BF16)], axis=1
+    )
+    back = dot(prod, wide[1])
+    cos, sin = twist[0], twist[1]
+    columns = []
+    for c in range(chans):
+        rows = back[c * devices : (c + 1) * devices]
+        br, bi = part(rows, 0), part(rows, 1)
+        columns.append(
+            jnp.concatenate(
+                [(br * cos - bi * sin).astype(BF16), (br * sin + bi * cos).astype(BF16)],
+                axis=0,
+            )
+        )
+    conv = dot(inv[...], jnp.concatenate(columns, axis=1))
+    for c in range(chans):
+        spread[pl.ds(c, devices, stride=chans), :] = part(conv, c)
+    fbuf[...] = (
+        spread[...].reshape(devices, chans, width)
+        + skipb[...] * gbuf[...].astype(F32)
+    ).astype(BF16)
+
+    def send_out(d, carry):
+        i = lax.rem(mine + d, lanes)
+        pltpu.make_async_remote_copy(
+            src_ref=fbuf.at[pl.ds(i * groups, groups)],
+            dst_ref=landed.at[:, side_rows(mine)],
+            send_sem=send_sem.at[4], recv_sem=recv_sem.at[4],
+            device_id=(i, side), device_id_type=MESH,
+        ).start()
+        return carry
+
+    lax.fori_loop(1, lanes, send_out, 0)
+    own_o = pltpu.make_async_copy(
+        fbuf.at[pl.ds(mine * groups, groups)], landed.at[:, side_rows(mine)], own_sem.at[3]
+    )
+    own_o.start()
 
     @pl.when(me < devices - 1)
     def _():
@@ -313,9 +308,7 @@
     pltpu.make_async_copy(others, others, recv_sem.at[3]).wait()
     own_q.wait()
     pltpu.make_async_copy(sent_f, sent_f, send_sem.at[4]).wait()
-    pltpu.make_async_copy(
-        fbuf.at[pl.ds(0, groups)], landed.at[:, pl.ds(0, chans)], own_sem.at[3]
-    ).wait()
+    own_o.wait()
     pltpu.make_async_copy(sent_f, sent_f, recv_sem.at[4]).wait()
     for g in range(groups):
         out[:, g * width : (g + 1) * width] = (
@@ -328,7 +321,7 @@
     channels, width = qkv.shape[1], qkv.shape[2]
     chans = channels // devices
     count = conv_taps.shape[2]
-    fwd, inv, wide, twist = tables(devices, width, chans)
+    fwd, inv, wide, twist = tables(devices, width)
     hbm = pl.BlockSpec(memory_space=pltpu.HBM)
     vmem = pl.BlockSpec(memory_space=pltpu.VMEM)
     per_side = lanes * chans
@@ -336,12 +329,13 @@
     return pl.pallas_call(
         functools.partial(kernel, lanes, groups, count - 1),
         out_shape=jax.ShapeDtypeStruct((per_side, groups * width), BF16),
-        in_specs=[hbm, hbm, hbm, vmem] + [hbm] * 4,
+        in_specs=[hbm] * 8,
         out_specs=vmem,
         scratch_shapes=[
             pltpu.VMEM(qkv.shape, BF16),
             pltpu.VMEM(filters.shape, F32),
             pltpu.VMEM((3, count, channels), F32),
+            pltpu.VMEM((1, per_side), F32),
             pltpu.VMEM(fwd.shape, BF16),
             pltpu.VMEM(inv.shape, BF16),
             pltpu.VMEM(wide.shape, BF16),
@@ -357,10 +351,10 @@
             pltpu.VMEM((devices, chans, width), BF16),
             pltpu.VMEM((groups, per_side, width), BF16),
             pltpu.VMEM((channels, 2 * width), F32),
-            pltpu.VMEM((2 * channels, width), BF16),
+            pltpu.VMEM((channels, width), F32),
             pltpu.VMEM((groups, per_side, width), BF16),
             pltpu.VMEM((groups, per_side, width), BF16),
-            pltpu.SemaphoreType.DMA((7,)),
+            pltpu.SemaphoreType.DMA((8,)),
             pltpu.SemaphoreType.DMA((4,)),
             pltpu.SemaphoreType.DMA((5,)),
             pltpu.SemaphoreType.DMA((5,)),
@@ -503,8 +497,7 @@
             and qkv.shape[2] == 128
             and (qkv.shape[1] // 16) % chans == 0
             and (lanes * chans) % (qkv.shape[1] // 16) == 0
-            and (lanes * groups) % 8 == 0
-            and 4 % groups == 0
+            and (lanes * groups) % 16 == 0
             and conv_taps.shape[2] <= 8
         )
         if fits:

time: 26.5 us -> 23.6 us (0.89)
  Pallas kernels: 24.8 us -> 21.8 us
    pallas_call x1, Pallas kernels: 24.8 us -> 21.8 us  [fused_local(): pl.pallas_call(functools.partial(kernel, lanes, groups, count - 1), out_s...]
where the time goes in v3:
time: 23.6 us; the launch traced here: 23.4 us
  Pallas kernels  21.8 us (92%)
  local copies, waits for them, and re-layouts  1.57 us (7%)
    pallas_call x1, Pallas kernels, fused_local(): pl.pallas_call(functools.partial(kernel, lanes, groups, count - 1), out_s...  21.8 us
    unnamed x1, local copies, waits for them, and re-layouts  1.57 us

profile of v3, /device:TPU:0, one launch (start us, length us, event | category | flops | bytes accessed | tf_op | source)
XLA Modules:
  0.0 23.4 jit_solution(18264641679706391126)
XLA Ops:
  0.0 21.8 %shard_map.82 = bf16[256,256]{1,0:T(8,128)(2,1)} custom-call(bf16[3,512,128]{2,1,0:T(8,128)(2,1)} %qkv.1, f32[3,7,512]{2,1,0:T(8,128)} %bitcast.2, f32[256,256]{1,0:T(8,128)} %filters.1, f32[1,256]{1,0:T(1,128)} %bitcast.3, bf16[64,32]{1,0:T(8,128)(2,1)} %constant.8.clone.fwd_hbm, bf16[32,64]{1,0:T(8,128)(2,1)} %constant.9.clone.inv_hbm, ...), custom_call_target="tpu_custom_call" | custom-call | tf_op jit(solution)/shard_map/pallas_call | solution.py:329
  21.8 1.6 %copy.10 = bf16[256,256]{1,0:T(8,128)(2,1)} copy(bf16[256,256]{1,0:T(8,128)(2,1)} %shard_map.82) | data formatting | bytes 262144

commit v4 on v3

--- a/solution.py
+++ b/solution.py
@@ -328,7 +328,7 @@
     halo = (3, channels * 8 // width, width)
     return pl.pallas_call(
         functools.partial(kernel, lanes, groups, count - 1),
-        out_shape=jax.ShapeDtypeStruct((per_side, groups * width), BF16),
+        out_shape=pltpu.VMEM((per_side, groups * width), BF16),
         in_specs=[hbm] * 8,
         out_specs=vmem,
         scratch_shapes=[
@@ -360,9 +360,17 @@
             pltpu.SemaphoreType.DMA((5,)),
         ],
         compiler_params=pltpu.CompilerParams(
-            collective_id=0, has_side_effects=True, vmem_limit_bytes=60 * 1024 * 1024
+            collective_id=0, has_side_effects=True, vmem_limit_bytes=24 * 1024 * 1024
         ),
-    )(qkv, conv_taps.transpose(0, 2, 1), filters, skip.reshape(1, -1), fwd, inv, wide, twist)
+    )(
+        *(
+            pltpu.with_memory_space_constraint(operand, pltpu.HBM)
+            for operand in (
+                qkv, conv_taps.transpose(0, 2, 1), filters, skip.reshape(1, -1),
+                fwd, inv, wide, twist,
+            )
+        )
+    )
 
 
 def from_behind(shard, axis, by):

time: 23.6 us -> 22 us (0.932)
  local copies, waits for them, and re-layouts: 1.57 us -> 0.66 us
  Pallas kernels: 21.8 us -> 21.1 us
    unnamed x1, local copies, waits for them, and re-layouts: 1.57 us -> 0.66 us
    pallas_call x1, Pallas kernels: 21.8 us -> 21.1 us  [fused_local(): pl.pallas_call(functools.partial(kernel, lanes, groups, count - 1), out_s...]
where the time goes in v4:
time: 22 us; the launch traced here: 21.8 us
  Pallas kernels  21.1 us (96%)
  local copies, waits for them, and re-layouts  0.66 us (3%)
    pallas_call x1, Pallas kernels, fused_local(): pl.pallas_call(functools.partial(kernel, lanes, groups, count - 1), out_s...  21.1 us
    unnamed x1, local copies, waits for them, and re-layouts  0.66 us

profile of v4, /device:TPU:0, one launch (start us, length us, event | category | flops | bytes accessed | tf_op | source)
XLA Modules:
  0.0 21.8 jit_solution(2697343999503149779)
XLA Ops:
  0.0 21.1 %shard_map.82 = bf16[256,256]{1,0:T(8,128)(2,1)S(1)} custom-call(bf16[3,512,128]{2,1,0:T(8,128)(2,1)} %qkv.1, f32[3,7,512]{2,1,0:T(8,128)} %bitcast.2, f32[256,256]{1,0:T(8,128)} %filters.1, f32[1,256]{1,0:T(1,128)} %bitcast.3, bf16[64,32]{1,0:T(8,128)(2,1)} %constant.8.clone.fwd_hbm, bf16[32,64]{1,0:T(8,128)(2,1)} %constant.9.clone.inv_hbm, ...), custom_call_target="tpu_custom_call" | custom-call | tf_op jit(solution)/shard_map/pallas_call | solution.py:329
  21.2 0.7 %copy.10 = bf16[256,256]{1,0:T(8,128)(2,1)} copy(bf16[256,256]{1,0:T(8,128)(2,1)S(1)} %shard_map.82) | data formatting | bytes 262144

commit v5 on v4

--- a/solution.py
+++ b/solution.py
@@ -39,7 +39,7 @@
     qkv, taps, filters, skip, fwd_hbm, inv_hbm, wide_hbm, twist_hbm,
     out,
     qin, fraw, tapv, skipv, fwd, inv, wide, twist,
-    halo_out, halo_in, tapc, tapb, skipb,
+    halo_out, halo_in, tapc, ptaps, feat, skipb,
     fsend, fbuf, gsend, gbuf, qland, hspec, spread, mbuf, landed,
     load_sem, own_sem, send_sem, recv_sem,
 ):
@@ -118,7 +118,8 @@
         ).start()
         return carry
 
-    lax.fori_loop(1, lanes, send_filters, 0)
+    lax.fori_loop(lanes // 2, lanes, send_filters, 0)
+    lax.fori_loop(1, lanes // 2, send_filters, 0)
     own_f = pltpu.make_async_copy(
         fsend.at[:, side_rows(mine)], fbuf.at[pl.ds(mine * groups, groups)], own_sem.at[0]
     )
@@ -131,13 +132,22 @@
         )
         tapc[s] = wide_taps.T
 
+    spot = lax.rem(lane, keep)
+    ptaps[...] = jnp.zeros_like(ptaps)
+
     @pl.loop(0, parts)
     def _(g):
         rows = pl.ds(pl.multiple_of(g * prows, prows), prows)
+        here = (lane >= keep * g) & (lane < keep * (g + 1))
         for s in range(3):
             columns = tapc[s, rows]
-            for i in range(reach + 1):
-                tapb[s, i, rows] = jnp.broadcast_to(columns[:, i : i + 1], (prows, width))
+            cur = qin[s, rows].astype(F32)
+            acc = columns[:, :1] * cur
+            for i in range(1, reach + 1):
+                tap = jnp.broadcast_to(columns[:, i : i + 1], (prows, width))
+                acc = acc + jnp.where(lane >= i, tap * pltpu.roll(cur, i, 1), 0.0)
+                ptaps[s, i - 1] = jnp.where(here & (spot < i), tap, ptaps[s, i - 1])
+            feat[s, rows] = acc
 
     pick = lax.broadcasted_iota(jnp.int32, (chans, per_side), 1) == (
         mine * chans + lax.broadcasted_iota(jnp.int32, (chans, per_side), 0)
@@ -154,48 +164,42 @@
     def _():
         halo_in[...] = jnp.zeros_like(halo_in)
 
+    added = []
+    for s in range(3):
+        tail = halo_in[s].astype(F32)
+        total = jnp.zeros((prows, width), F32)
+        for i in range(1, reach + 1):
+            total = total + ptaps[s, i - 1] * pltpu.roll(tail, width - keep + i, 1)
+        added.append(total)
+
     def feature(stream, g):
-        rows = pl.ds(pl.multiple_of(g * prows, prows), prows)
-        cur = qin[stream, rows].astype(F32)
-        prev = pltpu.roll(halo_in[stream].astype(F32), width - keep - keep * g, 1)
-        acc = tapb[stream, 0, rows] * cur
-        for i in range(1, reach + 1):
-            moved = pltpu.roll(jnp.where(lane >= width - i, prev, cur), i, 1)
-            acc = acc + tapb[stream, i, rows] * moved
-        return acc
-
-    fold = prows // chans
+        more = pltpu.roll(added[stream], (width - keep * g) % width, 1)
+        return feat[stream, g * prows : (g + 1) * prows] + jnp.where(lane < keep, more, 0.0)
+
+    for g in range(parts):
+        gsend[g * prows : (g + 1) * prows] = (feature(1, g) * feature(2, g)).astype(BF16)
+
+    def send_gated(d, carry):
+        t = lax.rem(me + d, devices)
+        i, j = t // groups, t % groups
+        row0 = pl.multiple_of(j * per_side + i * chans, chans)
+        pltpu.make_async_remote_copy(
+            src_ref=gsend.at[pl.ds(row0, chans)], dst_ref=gbuf.at[me],
+            send_sem=send_sem.at[2], recv_sem=recv_sem.at[2],
+            device_id=(i, j), device_id_type=MESH,
+        ).start()
+        return carry
+
+    lax.fori_loop(devices // 2, devices, send_gated, 0)
+    lax.fori_loop(1, devices // 2, send_gated, 0)
+    own_row = pl.multiple_of(side * per_side + mine * chans, chans)
+    own_g = pltpu.make_async_copy(gsend.at[pl.ds(own_row, chans)], gbuf.at[me], own_sem.at[1])
+    own_g.start()
+
     side_parts = per_side // prows
-
-    @pl.loop(0, parts)
-    def _(n):
-        g = lax.rem(n + me // fold, parts)
-        gate = (feature(1, g) * feature(2, g)).astype(BF16)
-        gsend[pl.ds(pl.multiple_of(g * prows, prows), prows)] = gate
-        j = g // side_parts
-        for f in range(fold):
-            i = (g % side_parts) * fold + f
-            src = gsend.at[pl.ds(pl.multiple_of(g * prows + f * chans, chans), chans)]
-            own = jnp.logical_and(i == mine, j == side)
-
-            @pl.when(own)
-            def _():
-                pltpu.make_async_copy(src, gbuf.at[me], own_sem.at[1]).start()
-
-            @pl.when(jnp.logical_not(own))
-            def _():
-                pltpu.make_async_remote_copy(
-                    src_ref=src, dst_ref=gbuf.at[me],
-                    send_sem=send_sem.at[2], recv_sem=recv_sem.at[2],
-                    device_id=(i, j), device_id_type=MESH,
-                ).start()
-
-    for j in range(groups):
-
-        @pl.loop(0, side_parts)
-        def _(n):
-            rows = pl.ds(pl.multiple_of(n * prows, prows), prows)
-            mbuf[j, rows] = feature(0, j * side_parts + n).astype(BF16)
+    for g in range(parts):
+        at = (g % side_parts) * prows
+        mbuf[g // side_parts, at : at + prows] = feature(0, g).astype(BF16)
 
     def send_query(d, carry):
         j = lax.rem(side + d, groups)
@@ -251,7 +255,7 @@
     hspec[...] = forward(fbuf)
 
     gated = gbuf.at[pl.ds(0, devices - 1)]
-    pltpu.make_async_copy(gsend.at[pl.ds(0, chans)], gbuf.at[me], own_sem.at[1]).wait()
+    own_g.wait()
     pltpu.make_async_copy(gated, gated, recv_sem.at[2]).wait()
 
     spec = forward(gbuf)
@@ -290,7 +294,8 @@
         ).start()
         return carry
 
-    lax.fori_loop(1, lanes, send_out, 0)
+    lax.fori_loop(lanes // 2, lanes, send_out, 0)
+    lax.fori_loop(1, lanes // 2, send_out, 0)
     own_o = pltpu.make_async_copy(
         fbuf.at[pl.ds(mine * groups, groups)], landed.at[:, side_rows(mine)], own_sem.at[3]
     )
@@ -343,7 +348,8 @@
             pltpu.VMEM(halo, BF16),
             pltpu.VMEM(halo, BF16),
             pltpu.VMEM((3, channels, width), F32),
-            pltpu.VMEM((3, count, channels, width), F32),
+            pltpu.VMEM((3, count - 1, halo[1], width), F32),
+            pltpu.VMEM((3, channels, width), F32),
             pltpu.VMEM((chans, width), F32),
             pltpu.VMEM((groups, per_side, width), BF16),
             pltpu.VMEM((devices, chans, width), BF16),

time: 22 us -> 23.9 us (1.086)
  Pallas kernels: 21.1 us -> 23.1 us
    pallas_call x1, Pallas kernels: 21.1 us -> 23.1 us  [fused_local(): pl.pallas_call(functools.partial(kernel, lanes, groups, count - 1), out_s...]
where the time goes in v5:
time: 23.9 us; the launch traced here: 23.7 us
  Pallas kernels  23.1 us (97%)
  local copies, waits for them, and re-layouts  0.66 us (3%)
    pallas_call x1, Pallas kernels, fused_local(): pl.pallas_call(functools.partial(kernel, lanes, groups, count - 1), out_s...  23.1 us
    unnamed x1, local copies, waits for them, and re-layouts  0.66 us

profile of v5, /device:TPU:0, one launch (start us, length us, event | category | flops | bytes accessed | tf_op | source)
XLA Modules:
  0.0 23.7 jit_solution(7398109149198233750)
XLA Ops:
  0.0 23.1 %shard_map.82 = bf16[256,256]{1,0:T(8,128)(2,1)S(1)} custom-call(bf16[3,512,128]{2,1,0:T(8,128)(2,1)} %qkv.1, f32[3,7,512]{2,1,0:T(8,128)} %bitcast.2, f32[256,256]{1,0:T(8,128)} %filters.1, f32[1,256]{1,0:T(1,128)} %bitcast.3, bf16[64,32]{1,0:T(8,128)(2,1)} %constant.8.clone.fwd_hbm, bf16[32,64]{1,0:T(8,128)(2,1)} %constant.9.clone.inv_hbm, ...), custom_call_target="tpu_custom_call" | custom-call | tf_op jit(solution)/shard_map/pallas_call | solution.py:334
  23.1 0.7 %copy.10 = bf16[256,256]{1,0:T(8,128)(2,1)} copy(bf16[256,256]{1,0:T(8,128)(2,1)S(1)} %shard_map.82) | data formatting | bytes 262144

commit v6 on v4

--- a/solution.py
+++ b/solution.py
@@ -39,7 +39,7 @@
     qkv, taps, filters, skip, fwd_hbm, inv_hbm, wide_hbm, twist_hbm,
     out,
     qin, fraw, tapv, skipv, fwd, inv, wide, twist,
-    halo_out, halo_in, tapc, tapb, skipb,
+    halo_out, halo_in, tapc, ptaps, fixes, feat, skipb,
     fsend, fbuf, gsend, gbuf, qland, hspec, spread, mbuf, landed,
     load_sem, own_sem, send_sem, recv_sem,
 ):
@@ -131,13 +131,25 @@
         )
         tapc[s] = wide_taps.T
 
-    @pl.loop(0, parts)
-    def _(g):
-        rows = pl.ds(pl.multiple_of(g * prows, prows), prows)
-        for s in range(3):
-            columns = tapc[s, rows]
-            for i in range(reach + 1):
-                tapb[s, i, rows] = jnp.broadcast_to(columns[:, i : i + 1], (prows, width))
+    spot = lax.rem(lane, keep)
+    ptaps[...] = jnp.zeros_like(ptaps)
+
+    def partial(streams):
+        @pl.loop(0, parts)
+        def _(g):
+            rows = pl.ds(pl.multiple_of(g * prows, prows), prows)
+            here = (lane >= keep * g) & (lane < keep * (g + 1))
+            for s in streams:
+                columns = tapc[s, rows]
+                cur = qin[s, rows].astype(F32)
+                acc = columns[:, :1] * cur
+                for i in range(1, reach + 1):
+                    tap = jnp.broadcast_to(columns[:, i : i + 1], (prows, width))
+                    acc = acc + jnp.where(lane >= i, tap * pltpu.roll(cur, i, 1), 0.0)
+                    ptaps[s, i - 1] = jnp.where(here & (spot < i), tap, ptaps[s, i - 1])
+                feat[s, rows] = acc
+
+    partial((1, 2))
 
     pick = lax.broadcasted_iota(jnp.int32, (chans, per_side), 1) == (
         mine * chans + lax.broadcasted_iota(jnp.int32, (chans, per_side), 0)
@@ -154,16 +166,20 @@
     def _():
         halo_in[...] = jnp.zeros_like(halo_in)
 
+    def correct(s):
+        tail = halo_in[s].astype(F32)
+        total = jnp.zeros((prows, width), F32)
+        for i in range(1, reach + 1):
+            total = total + ptaps[s, i - 1] * pltpu.roll(tail, width - keep + i, 1)
+        fixes[s] = total
+
     def feature(stream, g):
         rows = pl.ds(pl.multiple_of(g * prows, prows), prows)
-        cur = qin[stream, rows].astype(F32)
-        prev = pltpu.roll(halo_in[stream].astype(F32), width - keep - keep * g, 1)
-        acc = tapb[stream, 0, rows] * cur
-        for i in range(1, reach + 1):
-            moved = pltpu.roll(jnp.where(lane >= width - i, prev, cur), i, 1)
-            acc = acc + tapb[stream, i, rows] * moved
-        return acc
-
+        more = pltpu.roll(fixes[stream], lax.rem(width - keep * g, width), 1)
+        return feat[stream, rows] + jnp.where(lane < keep, more, 0.0)
+
+    correct(1)
+    correct(2)
     fold = prows // chans
     side_parts = per_side // prows
 
@@ -190,6 +206,8 @@
                     device_id=(i, j), device_id_type=MESH,
                 ).start()
 
+    partial((0,))
+    correct(0)
     for j in range(groups):
 
         @pl.loop(0, side_parts)
@@ -343,7 +361,9 @@
             pltpu.VMEM(halo, BF16),
             pltpu.VMEM(halo, BF16),
             pltpu.VMEM((3, channels, width), F32),
-            pltpu.VMEM((3, count, channels, width), F32),
+            pltpu.VMEM((3, count - 1, halo[1], width), F32),
+            pltpu.VMEM(halo, F32),
+            pltpu.VMEM((3, channels, width), F32),
             pltpu.VMEM((chans, width), F32),
             pltpu.VMEM((groups, per_side, width), BF16),
             pltpu.VMEM((devices, chans, width), BF16),

time: 22 us -> 21.5 us (0.977)
  Pallas kernels: 21.1 us -> 20.7 us
    pallas_call x1, Pallas kernels: 21.1 us -> 20.7 us  [fused_local(): pl.pallas_call(functools.partial(kernel, lanes, groups, count - 1), out_s...]
where the time goes in v6:
time: 21.5 us; the launch traced here: 21.4 us
  Pallas kernels  20.7 us (96%)
  local copies, waits for them, and re-layouts  0.66 us (3%)
    pallas_call x1, Pallas kernels, fused_local(): pl.pallas_call(functools.partial(kernel, lanes, groups, count - 1), out_s...  20.7 us
    unnamed x1, local copies, waits for them, and re-layouts  0.66 us

profile of v6, /device:TPU:0, one launch (start us, length us, event | category | flops | bytes accessed | tf_op | source)
XLA Modules:
  0.0 21.4 jit_solution(14553513999089690140)
XLA Ops:
  0.0 20.7 %shard_map.82 = bf16[256,256]{1,0:T(8,128)(2,1)S(1)} custom-call(bf16[3,512,128]{2,1,0:T(8,128)(2,1)} %qkv.1, f32[3,7,512]{2,1,0:T(8,128)} %bitcast.2, f32[256,256]{1,0:T(8,128)} %filters.1, f32[1,256]{1,0:T(1,128)} %bitcast.3, bf16[64,32]{1,0:T(8,128)(2,1)} %constant.8.clone.fwd_hbm, bf16[32,64]{1,0:T(8,128)(2,1)} %constant.9.clone.inv_hbm, ...), custom_call_target="tpu_custom_call" | custom-call | tf_op jit(solution)/shard_map/pallas_call | solution.py:347
  20.7 0.7 %copy.10 = bf16[256,256]{1,0:T(8,128)(2,1)} copy(bf16[256,256]{1,0:T(8,128)(2,1)S(1)} %shard_map.82) | data formatting | bytes 262144

commit v7 on v6

--- a/solution.py
+++ b/solution.py
@@ -108,8 +108,11 @@
     def _():
         halo_copy(after).start()
 
+    def near(d):
+        return (2 * (d % 2) - 1) * ((d + 1) // 2)
+
     def send_filters(d, carry):
-        i = lax.rem(mine + d, lanes)
+        i = lax.rem(mine + lanes + near(d), lanes)
         pltpu.make_async_remote_copy(
             src_ref=fsend.at[:, side_rows(i)],
             dst_ref=fbuf.at[pl.ds(mine * groups, groups)],
@@ -299,7 +302,7 @@
     ).astype(BF16)
 
     def send_out(d, carry):
-        i = lax.rem(mine + d, lanes)
+        i = lax.rem(mine + lanes + near(d), lanes)
         pltpu.make_async_remote_copy(
             src_ref=fbuf.at[pl.ds(i * groups, groups)],
             dst_ref=landed.at[:, side_rows(mine)],

time: 21.5 us -> 22.4 us (1.042)
  Pallas kernels: 20.7 us -> 21.6 us
    pallas_call x1, Pallas kernels: 20.7 us -> 21.6 us  [fused_local(): pl.pallas_call(functools.partial(kernel, lanes, groups, count - 1), out_s...]
where the time goes in v7:
time: 22.4 us; the launch traced here: 22.3 us
  Pallas kernels  21.6 us (96%)
  local copies, waits for them, and re-layouts  0.66 us (3%)
    pallas_call x1, Pallas kernels, fused_local(): pl.pallas_call(functools.partial(kernel, lanes, groups, count - 1), out_s...  21.6 us
    unnamed x1, local copies, waits for them, and re-layouts  0.66 us

profile of v7, /device:TPU:0, one launch (start us, length us, event | category | flops | bytes accessed | tf_op | source)
XLA Modules:
  0.0 22.3 jit_solution(991696604181004640)
XLA Ops:
  0.0 21.6 %shard_map.82 = bf16[256,256]{1,0:T(8,128)(2,1)S(1)} custom-call(bf16[3,512,128]{2,1,0:T(8,128)(2,1)} %qkv.1, f32[3,7,512]{2,1,0:T(8,128)} %bitcast.2, f32[256,256]{1,0:T(8,128)} %filters.1, f32[1,256]{1,0:T(1,128)} %bitcast.3, bf16[64,32]{1,0:T(8,128)(2,1)} %constant.8.clone.fwd_hbm, bf16[32,64]{1,0:T(8,128)(2,1)} %constant.9.clone.inv_hbm, ...), custom_call_target="tpu_custom_call" | custom-call | tf_op jit(solution)/shard_map/pallas_call | solution.py:350
  21.6 0.7 %copy.10 = bf16[256,256]{1,0:T(8,128)(2,1)} copy(bf16[256,256]{1,0:T(8,128)(2,1)S(1)} %shard_map.82) | data formatting | bytes 262144
